TPU v7x, 256 devices: a whole 4x4x8 slice. The times are simulated.
256 devices in a mesh: dp: 8 (over x, core), expert: 32 (over y, z).
Axes of the slice: x: 4, y: 4, z: 8, core: 2. Of those that a mesh axis runs over, the one named last changes fastest.
Arguments:
- cache_lat: bfloat16 [12288, 64, 512], P(('dp', 'expert')), may hold values from -6 to 6
- cache_rope: bfloat16 [12288, 4096], P(('dp', 'expert')), may hold values from -6 to 6
- page_scale: bfloat16 [12288], P(('dp', 'expert')), may hold values from 0.5 to 2
- move_list: int32 [256, 8, 4], P(('dp', 'expert')), may hold values from 0 to 47
- page_table: int32 [512, 32], P(('dp', 'expert')), may hold values from 0 to 79, as said below
- lengths: int32 [512], P(('dp', 'expert')), may hold values from 961 to 2048, as said below
- q_lat: bfloat16 [512, 2, 64, 512], P(('dp', 'expert')), may hold values from -72 to 72
- q_rope: bfloat16 [512, 2, 64, 64], P(('dp', 'expert')), may hold values from -12 to 12
- new_lat: bfloat16 [512, 2, 512], P(('dp', 'expert')), may hold values from -6 to 6
- new_rope: bfloat16 [512, 2, 64], P(('dp', 'expert')), may hold values from -6 to 6
- w_uv: bfloat16 [64, 512, 128], P('expert'), may hold values from -6 to 6
- w_out: bfloat16 [8192, 3584], P('expert'), may hold values from -0.0625 to 0.0625
- residual: bfloat16 [1024, 3584], P(('dp', 'expert')), may hold values from -400 to 400
- norm_gain: float32 [3584], replicated, may hold values from 0.1 to 1.9
- w_router: bfloat16 [3584, 32], replicated, may hold values from -0.09375 to 0.09375
- routes: int32 [1024, 8], P(('dp', 'expert')), may hold values from 0 to 31, all different within a row; in each aligned block of 4 rows (0 to 3, 4 to 7, ...) at most 2 rows name the same one
- w_gate: bfloat16 [32, 3584, 2048], P('expert', None, 'dp'), may hold values from -0.09375 to 0.09375
- w_up: bfloat16 [32, 3584, 2048], P('expert', None, 'dp'), may hold values from -0.09375 to 0.09375
- w_down: bfloat16 [32, 2048, 3584], P('expert', 'dp'), may hold values from -0.125 to 0.125
Outputs:
- attn_out: bfloat16 [1024, 3584], P(('dp', 'expert'))
- moe_out: bfloat16 [1024, 3584], P(('dp', 'expert'))
Inputs may be any that keep to these rules, and one draw needn't show every extreme that they name: `lengths`: cached tokens of a rollout besides its 2 new ones; some rollout holds 2048. `page_table`: a rollout names no page index twice. `routes`: among the rows of one device no expert is named more than 2 times; some expert is named exactly 2 times.
All inputs are finite; a program needn't handle non-finite values.
Results may differ from a plain program's by a relative error of at most 0.03.
Values may be sent and summed in bfloat16 or wider, within the bound.
A program may use at most 128 MiB of HBM per device.

v0:
```python
import jax
import jax.numpy as jnp
from jax import lax
from jax.sharding import PartitionSpec as P

SCORE_SCALE = 0.07216878364870322
ROUTE_SCALE = 2.5
NORM_EPS = 1e-06


def slot_masks(weight_table, capacity):
    chosen = (weight_table > 0.0).astype(jnp.int32)
    earlier = jnp.cumsum(chosen, axis=-2) - chosen
    slot_ids = jnp.arange(capacity, dtype=jnp.int32)
    return (earlier[..., None] == slot_ids) & (chosen[..., None] > 0)


def body(
    cache_lat,
    cache_rope,
    page_scale,
    move_list,
    page_table,
    lengths,
    q_lat,
    q_rope,
    new_lat,
    new_rope,
    w_uv,
    w_out,
    residual,
    norm_gain,
    w_router,
    routes,
    w_gate,
    w_up,
    w_down,
):
    dp_count = lax.axis_size("dp")
    page_len = cache_lat.shape[1]
    latent_dim = cache_lat.shape[2]
    rope_dim = q_rope.shape[3]
    moves_each = move_list.shape[2]
    rollouts = q_lat.shape[0]
    next_count = q_lat.shape[1]
    table_len = page_table.shape[1]
    model_dim = residual.shape[1]
    highest = lax.Precision.HIGHEST
    picked = move_list[0]
    sent = (cache_lat[picked], cache_rope[picked], page_scale[picked])
    got_lat, got_rope, got_scale = (
        lax.all_to_all(sent[0], "dp", split_axis=0, concat_axis=0, tiled=True),
        lax.all_to_all(sent[1], "dp", split_axis=0, concat_axis=0, tiled=True),
        lax.all_to_all(sent[2], "dp", split_axis=0, concat_axis=0, tiled=True),
    )
    view_lat = jnp.concatenate(
        [cache_lat, got_lat.reshape(dp_count * moves_each, page_len, latent_dim)], axis=0
    )
    view_rope = jnp.concatenate([cache_rope, got_rope.reshape(dp_count * moves_each, -1)], axis=0)
    view_scale = jnp.concatenate([page_scale, got_scale.reshape(-1)], axis=0)
    cached = table_len * page_len
    keys_lat = view_lat[page_table].reshape(rollouts, cached, latent_dim)
    keys_rope = view_rope[page_table].reshape(rollouts, cached, rope_dim)
    page_factor = view_scale[page_table].astype(jnp.float32)
    token_scale = jnp.broadcast_to(
        page_factor[:, :, None], (rollouts, table_len, page_len)
    ).reshape(rollouts, cached)
    old_scores = jnp.einsum("rphl,rtl->rpht", q_lat, keys_lat, preferred_element_type=jnp.float32)
    old_scores = old_scores + jnp.einsum(
        "rphk,rtk->rpht", q_rope, keys_rope, preferred_element_type=jnp.float32
    )
    old_scores = old_scores * (token_scale * SCORE_SCALE)[:, None, None, :]
    live = jnp.arange(cached, dtype=jnp.int32)[None, :] < lengths[:, None]
    old_scores = jnp.where(live[:, None, None, :], old_scores, -jnp.inf)
    new_scores = jnp.einsum("rphl,rul->rphu", q_lat, new_lat, preferred_element_type=jnp.float32)
    new_scores = new_scores + jnp.einsum(
        "rphk,ruk->rphu", q_rope, new_rope, preferred_element_type=jnp.float32
    )
    new_scores = new_scores * SCORE_SCALE
    causal = jnp.arange(next_count)[None, :] <= jnp.arange(next_count)[:, None]
    new_scores = jnp.where(causal[None, :, None, :], new_scores, -jnp.inf)
    peak = jnp.maximum(jnp.max(old_scores, -1), jnp.max(new_scores, -1))
    old_exp = jnp.exp(old_scores - peak[..., None])
    new_exp = jnp.exp(new_scores - peak[..., None])
    total = jnp.sum(old_exp, -1) + jnp.sum(new_exp, -1)
    old_weights = (old_exp / total[..., None] * token_scale[:, None, None, :]).astype(jnp.bfloat16)
    new_weights = (new_exp / total[..., None]).astype(jnp.bfloat16)
    latent_sum = jnp.einsum(
        "rpht,rtl->rphl", old_weights, keys_lat, preferred_element_type=jnp.float32
    )
    latent_sum = latent_sum + jnp.einsum(
        "rphu,rul->rphl", new_weights, new_lat, preferred_element_type=jnp.float32
    )
    latent_out = latent_sum.astype(jnp.bfloat16)
    head_group = lax.all_to_all(latent_out, "expert", split_axis=2, concat_axis=0, tiled=True)
    head_values = jnp.einsum(
        "rphl,hlv->rphv", head_group, w_uv, preferred_element_type=jnp.float32
    ).astype(jnp.bfloat16)
    value_rows = head_values.reshape(head_values.shape[0] * next_count, -1)
    attn_sum = lax.psum_scatter(
        jnp.dot(value_rows, w_out, preferred_element_type=jnp.float32).astype(jnp.bfloat16),
        "expert",
        scatter_dimension=0,
        tiled=True,
    ).astype(jnp.float32)
    attn_out = attn_sum.astype(jnp.bfloat16)
    hidden = (residual.astype(jnp.float32) + attn_sum).astype(jnp.bfloat16)
    hidden_f = hidden.astype(jnp.float32)
    normed = (
        hidden_f
        * lax.rsqrt(jnp.mean(hidden_f * hidden_f, -1, keepdims=True) + NORM_EPS)
        * norm_gain
    ).astype(jnp.bfloat16)
    logits = jnp.dot(normed, w_router, preferred_element_type=jnp.float32)
    expert_total = w_router.shape[1]
    top_count = routes.shape[1]
    onehot = routes[:, :, None] == jnp.arange(expert_total, dtype=jnp.int32)[None, None, :]
    selected = jnp.sum(jnp.where(onehot, logits[:, None, :], jnp.float32(0.0)), -1)
    sig = jax.nn.sigmoid(selected)
    gates = ROUTE_SCALE * sig / jnp.sum(sig, -1, keepdims=True)
    weight_table = jnp.sum(jnp.where(onehot, gates[:, :, None], jnp.float32(0.0)), 1)
    capacity = min(2 * rollouts, max(2, 4 * rollouts * top_count // expert_total))
    own_slots = slot_masks(weight_table, capacity)
    send_rows = jnp.einsum(
        "tec,td->ecd", own_slots.astype(jnp.bfloat16), normed, preferred_element_type=jnp.float32
    ).astype(jnp.bfloat16)
    arrived = lax.all_to_all(send_rows, "expert", split_axis=0, concat_axis=0, tiled=True)
    grouped = lax.all_gather(arrived, "dp", axis=1, tiled=True)
    flat_rows = grouped.reshape(-1, model_dim)
    gate_part = jnp.dot(flat_rows, w_gate[0], preferred_element_type=jnp.float32)
    up_part = jnp.dot(flat_rows, w_up[0], preferred_element_type=jnp.float32)
    expert_hidden = (jax.nn.silu(gate_part) * up_part).astype(jnp.bfloat16)
    partial_out = jnp.dot(expert_hidden, w_down[0], preferred_element_type=jnp.float32)
    partial_out = partial_out.reshape(expert_total, dp_count, capacity, model_dim)
    group_table = lax.all_gather(weight_table, "dp", axis=0, tiled=True)
    group_table = group_table.reshape(dp_count, -1, expert_total)
    group_slots = slot_masks(group_table, capacity)
    combine_weights = jnp.where(group_slots, group_table[..., None], jnp.float32(0.0))
    returned = lax.all_to_all(
        partial_out.astype(jnp.bfloat16), "expert", split_axis=0, concat_axis=0, tiled=True
    ).astype(partial_out.dtype)
    mixed = jnp.einsum("ktec,ekcd->ktd", combine_weights, returned, precision=highest)
    moe_sum = lax.psum_scatter(
        mixed.astype(jnp.bfloat16), "dp", scatter_dimension=0, tiled=True
    ).astype(jnp.float32)[0]
    return (attn_out, moe_sum.astype(jnp.bfloat16))


def solution(mesh):
    return jax.shard_map(
        body,
        mesh=mesh,
        in_specs=(
            P(("dp", "expert"), None, None),
            P(("dp", "expert"), None),
            P(("dp", "expert")),
            P(("dp", "expert"), None, None),
            P(("dp", "expert"), None),
            P(("dp", "expert")),
            P(("dp", "expert"), None, None, None),
            P(("dp", "expert"), None, None, None),
            P(("dp", "expert"), None, None),
            P(("dp", "expert"), None, None),
            P("expert", None, None),
            P("expert", None),
            P(("dp", "expert"), None),
            P(),
            P(),
            P(("dp", "expert"), None),
            P("expert", None, "dp"),
            P("expert", None, "dp"),
            P("expert", "dp", None),
        ),
        out_specs=(P(("dp", "expert"), None), P(("dp", "expert"), None)),
        check_vma=False,
    )
```

profile of v0, /device:TPU:1, one launch (start us, length us, event | category | flops | bytes accessed | tf_op | source)
XLA Modules:
  0.0 483.6 jit_solution(2590850772361727930)
XLA Ops:
  10.3 6.5 %all-to-all-start.2 = ((bf16[8,1,4]{2,1,0:T(2,128)(2,1)}), bf16[8,1,4]{2,1,0:T(2,128)(2,1)S(1)}, u32[]{:S(2)}, u32[]{:S(2)}) async-start(bf16[8,1,4]{2,1,0:T(2,128)(2,1)} %all_to_all.41), calls=%async_computation.2 | async-start | bytes 8192 | tf_op jit(solution)/shard_map/all_to_all | solution.py:54
  18.5 2.8 all-to-all-done.2
  21.3 4.0 all-to-all-start.1
  25.3 4.0 gather_fusion
  29.6 2.2 all-to-all-done.1
  31.8 5.4 %all-to-all-start = ((bf16[8,4,64,512]{3,2,1,0:T(8,128)(2,1)}), bf16[8,4,64,512]{3,2,1,0:T(8,128)(2,1)}, u32[]{:S(2)}, u32[]{:S(2)}) async-start(bf16[8,4,64,512]{3,2,1,0:T(8,128)(2,1)} %bitcast.94), calls=%async_computation | async-start | bytes 4194304 | tf_op jit(solution)/shard_map/all_to_all | solution.py:52
  40.7 1.7 fusion.22
  42.4 21.2 %all-to-all-done = bf16[8,4,64,512]{3,2,1,0:T(8,128)(2,1)} async-done(((bf16[8,4,64,512]{3,2,1,0:T(8,128)(2,1)}), bf16[8,4,64,512]{3,2,1,0:T(8,128)(2,1)}, u32[]{:S(2)}, u32[]{:S(2)}) %all-to-all-start) | async-done | bytes 2097184 | tf_op jit(solution)/shard_map/all_to_all | solution.py:52
  63.7 5.3 %pad_maximum_fusion = bf16[80,64,512]{2,1,0:T(8,128)(2,1)} fusion(bf16[32,64,512]{2,1,0:T(8,128)(2,1)} %bitcast.2, bf16[48,64,512]{2,1,0:T(8,128)(2,1)} %param.19), kind=kLoop, calls=%fused_computation.7 | loop fusion | flops 2621440 | bytes 10485760 | tf_op jit(solution)/shard_map/concatenate | solution.py:56
  68.9 5.3 %gather_fusion.1 = bf16[64,64,512]{2,1,0:T(8,128)(2,1)} fusion(bf16[80,64,512]{2,1,0:T(8,128)(2,1)} %pad_maximum_fusion, s32[1024]{0:T(1024)S(1)} %pad_clamp_fusion), kind=kCustom, calls=%fused_computation.1 | custom fusion | bytes 8388864 | tf_op jit(solution)/shard_map/gather | solution.py:62
  74.3 4.6 fusion.60
  80.8 20.0 %all_to_all.48 = bf16[2,2,64,512]{3,1,0,2:T(2,128)(2,1)S(1)} all-to-all(bf16[2,2,64,512]{3,1,0,2:T(2,128)(2,1)S(1)} %copy.44), channel_id=1, replica_groups=mesh['dp'=8,'expert'=32] {'expert'}, dimensions={2} | all-to-all | bytes 524288 | tf_op jit(solution)/shard_map/all_to_all | solution.py:95
  101.5 2.9 convolution_convert_fusion.1
  105.8 140.5 %all-reduce.5.cloned.1.call-done = bf16[128,3584]{1,0:T(8,128)(2,1)} async-done(((bf16[128,3584]{1,0:T(8,128)(2,1)}), bf16[128,3584]{1,0:T(8,128)(2,1)}) %all-reduce.5.cloned.1.call-update) | async-done | bytes 917520
  248.8 16.1 %all_to_all.49 = bf16[32,2,3584]{2,1,0:T(2,128)(2,1)S(1)} all-to-all(bf16[32,2,3584]{2,1,0:T(2,128)(2,1)S(1)} %copy.47), channel_id=1, replica_groups=mesh['dp'=8,'expert'=32] {'expert'}, dimensions={0} | all-to-all | bytes 917504 | tf_op jit(solution)/shard_map/all_to_all | solution.py:127
  265.8 36.0 %all-gather.3.cloned.1.call-done = bf16[32,16,3584]{2,0,1:T(8,128)(2,1)} async-done(((bf16[32,2,3584]{2,0,1:T(8,128)(2,1)}), bf16[32,16,3584]{2,0,1:T(8,128)(2,1)}) %all-gather.3.cloned.1.call-update) | async-done | bytes 3670032 | tf_op jit(solution)/shard_map/all_gather | solution.py:128
  301.7 4.2 copy.49
  309.8 5.6 %copy.51 = bf16[32,8,2,3584]{3,2,1,0:T(2,128)(2,1)} copy(bf16[32,8,2,3584]{3,0,2,1:T(8,128)(2,1)S(1)} %convolution_convert_fusion) | data formatting | bytes 7340032 | tf_op jit(solution)/shard_map/convert_element_type | solution.py:140
  315.4 9.7 %all-to-all-start.5 = ((bf16[32,8,2,3584]{3,2,1,0:T(2,128)(2,1)}), bf16[32,8,2,3584]{3,2,1,0:T(2,128)(2,1)}, u32[]{:S(2)}, u32[]{:S(2)}) async-start(bf16[32,8,2,3584]{3,2,1,0:T(2,128)(2,1)} %copy.51), calls=%async_computation.5 | async-start | bytes 7340032 | tf_op jit(solution)/shard_map/all_to_all | solution.py:139
  325.2 11.8 %all-gather = f32[8,4,32]{2,1,0:T(4,128)S(1)} all-gather(f32[1,4,32]{2,1,0:T(4,128)S(1)} %bitcast.100), channel_id=1, replica_groups=mesh['dp'=8,'expert'=32] {'dp'}, dimensions={0}, use_global_device_ids=true | all-gather | bytes 4608 | tf_op jit(solution)/shard_map/all_gather | solution.py:135
  337.1 69.6 %all-to-all-done.5 = bf16[32,8,2,3584]{3,2,1,0:T(2,128)(2,1)} async-done(((bf16[32,8,2,3584]{3,2,1,0:T(2,128)(2,1)}), bf16[32,8,2,3584]{3,2,1,0:T(2,128)(2,1)}, u32[]{:S(2)}, u32[]{:S(2)}) %all-to-all-start.5) | async-done | bytes 3670048 | tf_op jit(solution)/shard_map/all_to_all | solution.py:139
  406.6 5.9 %fusion = bf16[8,4,3584]{2,1,0:T(4,128)(2,1)} fusion(bf16[32,8,2,3584]{3,2,1,0:T(2,128)(2,1)} %all-to-all-done.5, f32[8,4,32]{2,1,0:T(4,128)S(1)} %all-gather, s32[8,4,32]{2,1,0:T(4,128)S(1)} %fusion.56, pred[8,4,32]{2,1,0:T(4,128)(4,1)S(1)} %get-tuple-element.4), kind=kOutput, calls=%fused_computation.11 | convolution fusion | flops 88201216 | bytes 3908608 | tf_op jit(solution)/shard_map/ktec,ekcd->ktd/dot_general | solution.py:142
  413.3 61.7 %all-reduce.7.cloned.1.call-done = bf16[8,4,3584]{2,1,0:T(4,128)(2,1)} async-done(((bf16[8,4,3584]{2,1,0:T(4,128)(2,1)}), bf16[8,4,3584]{2,1,0:T(4,128)(2,1)}) %all-reduce.7.cloned.1.call-update) | async-done | bytes 229392
  475.0 2.1 dynamic-slice_bitcast_fusion
  (108 shorter events, 19.7 us)
Async XLA Ops:
  7.2 301.5 %copy-start = (bf16[1,256,3584]{2,1,0:T(8,128)(2,1)S(1)}, bf16[1,256,3584]{2,1,0:T(8,128)(2,1)}, u32[]{:S(2)}) copy-start(bf16[1,256,3584]{2,1,0:T(8,128)(2,1)} %param.37) | copy-start | bytes 5505028
  7.2 9.6 %copy-start.13 = (s32[2,32]{1,0:T(2,128)S(1)}, s32[2,32]{1,0:T(2,128)}, u32[]{:S(2)}) copy-start(s32[2,32]{1,0:T(2,128)} %param.23) | copy-start | bytes 772
  7.2 9.6 %copy-start.3 = (bf16[48,4096]{1,0:T(8,128)(2,1)S(1)}, bf16[48,4096]{1,0:T(8,128)(2,1)}, u32[]{:S(2)}) copy-start(bf16[48,4096]{1,0:T(8,128)(2,1)} %param.20) | copy-start | bytes 1179652
  8.2 9.3 %copy-start.4 = (bf16[2,2,64,512]{3,2,1,0:T(8,128)(2,1)S(1)}, bf16[2,2,64,512]{3,2,1,0:T(8,128)(2,1)}, u32[]{:S(2)}) copy-start(bf16[2,2,64,512]{3,2,1,0:T(8,128)(2,1)} %param.25) | copy-start | bytes 786436
  8.2 9.3 %copy-start.10 = (bf16[2,2,512]{2,1,0:T(2,128)(2,1)S(1)}, bf16[2,2,512]{2,1,0:T(2,128)(2,1)}, u32[]{:S(2)}) copy-start(bf16[2,2,512]{2,1,0:T(2,128)(2,1)} %param.27) | copy-start | bytes 12292
  10.3 11.0 %all-to-all-start.2 = ((bf16[8,1,4]{2,1,0:T(2,128)(2,1)}), bf16[8,1,4]{2,1,0:T(2,128)(2,1)S(1)}, u32[]{:S(2)}, u32[]{:S(2)}) async-start(bf16[8,1,4]{2,1,0:T(2,128)(2,1)} %all_to_all.41), calls=%async_computation.2 | async-start | bytes 8192 | tf_op jit(solution)/shard_map/all_to_all | solution.py:54
  21.3 10.5 %all-to-all-start.1 = ((bf16[8,4,4096]{2,1,0:T(4,128)(2,1)}), bf16[8,4,4096]{2,1,0:T(4,128)(2,1)S(1)}, u32[]{:S(2)}, u32[]{:S(2)}) async-start(bf16[8,4,4096]{2,1,0:T(4,128)(2,1)} %reshape.215), calls=%async_computation.1 | async-start | bytes 524288 | tf_op jit(solution)/shard_map/all_to_all | solution.py:53
  31.8 5.4 %copy-start.14 = (s32[2]{0:T(128)S(1)}, s32[2]{0:T(128)}, u32[]{:S(2)}) copy-start(s32[2]{0:T(128)} %param.24) | copy-start | bytes 28
  31.8 5.6 %copy-start.1 = (bf16[48]{0:T(256)(128)(2,1)S(1)}, bf16[48]{0:T(256)(128)(2,1)}, u32[]{:S(2)}) copy-start(bf16[48]{0:T(256)(128)(2,1)} %param.21) | copy-start | bytes 292
  31.8 31.8 %all-to-all-start = ((bf16[8,4,64,512]{3,2,1,0:T(8,128)(2,1)}), bf16[8,4,64,512]{3,2,1,0:T(8,128)(2,1)}, u32[]{:S(2)}, u32[]{:S(2)}) async-start(bf16[8,4,64,512]{3,2,1,0:T(8,128)(2,1)} %bitcast.94), calls=%async_computation | async-start | bytes 4194304 | tf_op jit(solution)/shard_map/all_to_all | solution.py:52
  37.2 209.0 %all-reduce.5.cloned.1.call-start = ((), (), s32[]{:S(2)}) async-start(), calls=%async_computation.7 | async-start | bytes 1835008
  68.9 5.4 %copy-start.5 = (bf16[2,2,64,512]{3,2,1,0:T(8,128)(2,1)S(1)}, bf16[2,2,64,512]{3,2,1,0:T(8,128)(2,1)}, u32[]{:S(2)}) copy-start(bf16[2,2,64,512]{3,2,1,0:T(8,128)(2,1)} %param.25) | copy-start | bytes 786436
  74.3 5.1 %copy-start.2 = (bf16[64,64,512]{2,1,0:T(8,128)(2,1)S(1)}, bf16[64,64,512]{2,1,0:T(8,128)(2,1)}, u32[]{:S(2)}) copy-start(bf16[64,64,512]{2,1,0:T(8,128)(2,1)} %gather_fusion.1) | copy-start | bytes 12582916
  80.3 20.9 %copy-start.6 = (bf16[2,512,128]{2,1,0:T(8,128)(2,1)S(1)}, bf16[2,512,128]{2,1,0:T(8,128)(2,1)}, u32[]{:S(2)}) copy-start(bf16[2,512,128]{2,1,0:T(8,128)(2,1)} %param.29) | copy-start | bytes 786436
  101.4 144.8 %copy-start.7 = (bf16[4,3584]{1,0:T(4,128)(2,1)S(1)}, bf16[4,3584]{1,0:T(4,128)(2,1)}, u32[]{:S(2)}) copy-start(bf16[4,3584]{1,0:T(4,128)(2,1)} %param.31) | copy-start | bytes 86020
  101.4 145.8 %copy-start.11 = (f32[3584]{0:T(1024)S(1)}, f32[3584]{0:T(1024)}, u32[]{:S(2)}) copy-start(f32[3584]{0:T(1024)} %param.32) | copy-start | bytes 43012
  101.4 145.8 %copy-start.17 = (bf16[3584,32]{0,1:T(8,128)(2,1)S(1)}, bf16[3584,32]{0,1:T(8,128)(2,1)}, u32[]{:S(2)}) copy-start(bf16[3584,32]{0,1:T(8,128)(2,1)} %param.33) | copy-start | bytes 688132
  101.5 145.9 %copy-start.12 = (s32[4,8]{1,0:T(4,128)S(1)}, s32[4,8]{1,0:T(4,128)}, u32[]{:S(2)}) copy-start(s32[4,8]{1,0:T(4,128)} %param.34) | copy-start | bytes 388
  104.5 197.3 %all-gather.3.cloned.1.call-start = ((), (), s32[]{:S(2)}) async-start(), calls=%async_computation.6 | async-start | bytes 4128768 | tf_op jit(solution)/shard_map/all_gather | solution.py:128
  247.2 58.7 %copy-start.8 = (bf16[4,3584]{1,0:T(4,128)(2,1)}, bf16[4,3584]{1,0:T(4,128)(2,1)S(1)}, u32[]{:S(2)}) copy-start(bf16[4,3584]{1,0:T(4,128)(2,1)S(1)} %get-tuple-element.3) | copy-start | bytes 86020
  301.7 4.2 copy-start.15
  315.4 91.2 %all-to-all-start.5 = ((bf16[32,8,2,3584]{3,2,1,0:T(2,128)(2,1)}), bf16[32,8,2,3584]{3,2,1,0:T(2,128)(2,1)}, u32[]{:S(2)}, u32[]{:S(2)}) async-start(bf16[32,8,2,3584]{3,2,1,0:T(2,128)(2,1)} %copy.51), calls=%async_computation.5 | async-start | bytes 7340032 | tf_op jit(solution)/shard_map/all_to_all | solution.py:139
  325.1 149.9 %all-reduce.7.cloned.1.call-start = ((), (), s32[]{:S(2)}) async-start(), calls=%async_computation.8 | async-start | bytes 458752
  337.0 75.6 %copy-start.19 = (u32[256]{0:T(256)S(1)}, u32[256]{0:T(256)}, u32[]{:S(2)}) copy-start(u32[256]{0:T(256)} %constant.57) | copy-start | bytes 3076
  (4 other events, 13.0 us)
Sparse Core Ops, SparseCore 0:
  104.6 141.5 all-reduce.4
  265.9 35.8 all-gather.2
  412.7 62.2 all-reduce.6
where the time goes:
time: 484 us
  waiting for transfers between devices  334 us (69%)
  blocking collectives  47.9 us (10%)
  local copies, waits for them, and re-layouts  32 us (7%)
  starting transfers between devices  25.6 us (5%)
  matrix products  20.8 us (4%)
  between operations  14.9 us (3%)
  other arithmetic  8.38 us (2%)
    unnamed x5, waiting for transfers between devices  202 us
    all_to_all x1, waiting for transfers between devices, body(): lax.all_to_all(partial_out.astype(jnp.bfloat16), 'expert', split_axis=0,...  69.6 us
    all_gather x1, waiting for transfers between devices, body(): grouped = lax.all_gather(arrived, 'dp', axis=1, tiled=True)  36 us
    all_to_all x1, waiting for transfers between devices, body(): lax.all_to_all(sent[0], 'dp', split_axis=0, concat_axis=0, tiled=True)  21.2 us
    all_to_all x1, blocking collectives, body(): lax.all_to_all(latent_out, 'expert', split_axis=2, concat_axis=0, tiled=T...  20 us
    all_to_all x1, blocking collectives, body(): lax.all_to_all(send_rows, 'expert', split_axis=0, concat_axis=0, tiled=True)  16.1 us
    all_gather x1, blocking collectives, body(): group_table = lax.all_gather(weight_table, 'dp', axis=0, tiled=True)  11.8 us
    all_to_all x1, starting transfers between devices, body(): lax.all_to_all(partial_out.astype(jnp.bfloat16), 'expert', split_axis=0,...  9.68 us
  transfers between devices with their start and end apart: 7, of which 7 were waited for; matrix products, arithmetic and copies ran while one was open for 3% of the time, Pallas kernels for 0%

commit v1 on v0

v1 whole, which is shorter than its diff:
```python
import jax
import jax.numpy as jnp
from jax import lax
from jax.experimental import pallas as pl
from jax.experimental.pallas import tpu as pltpu
from jax.sharding import PartitionSpec as P

MESH = pl.DeviceIdType.MESH
SCORE_SCALE = 0.07216878364870322
ROUTE_SCALE = 2.5
NORM_EPS = 1e-06
NEG = -1e30
F32 = jnp.float32
BF16 = jnp.bfloat16
D = 3584
CH = 512
NK = 7
HALF = 1792


def dot(a, b):
    return lax.dot_general(a, b, (((1,), (0,)), ((), ())), preferred_element_type=F32)


def dot_nt(a, b):
    return lax.dot_general(a, b, (((1,), (1,)), ((), ())), preferred_element_type=F32)


def iota(shape, dim):
    return lax.broadcasted_iota(jnp.int32, shape, dim)


def kernel(
    mv_ref, ps_ref, lat_hbm, rope_ref, aux_ref, q_ref, qr_ref, nl_ref, nr_ref,
    wuv_hbm, wout_hbm, res_ref, gain_ref, wr_ref, rt_ref, wg_hbm, wu_hbm, wd_hbm,
    attn_ref, moe_ref,
    lat_v, wuv, wout, wg, wu, wd,
    slat, srope, rlat, rrope, newk, newr, q_l, q_r, m_s, l_s, o_s,
    so, ro, hv_s, pf, ps1, pr1, s_f, d_f, sp2, pr2, al_f, res_l, gain_l,
    q_s, qt_s, sd, rd, t_f, xr, pp, sr, ss, hb, hr, fb, fr, sret, rret,
    lsem, pg_s, pg_r, o_ss, o_rs, p1_s, p1_r, p2_s, p2_r, d_ss, d_rs, ag_s, ag_r, rs_s, rs_r, b_ss, b_rs,
):
    i = lax.axis_index("dp")
    j = lax.axis_index("expert")
    x, c, y, z = i // 2, i % 2, j // 8, j % 8

    def dp_to(dx, dc):
        return (((x + dx) % 4) * 2 + (c + dc) % 2, j)

    def ex_at(dy, dz):
        return ((y + dy + 4) % 4) * 8 + (z + dz + 8) % 8

    def rcopy(src, dst, send, recv, dev):
        return pltpu.make_async_remote_copy(
            src_ref=src, dst_ref=dst, send_sem=send, recv_sem=recv, device_id=dev, device_id_type=MESH
        )

    right, left, sib = dp_to(1, 0), dp_to(3, 0), dp_to(0, 1)

    loads = [
        pltpu.make_async_copy(a, b, lsem.at[n])
        for n, (a, b) in enumerate(
            [(lat_hbm, lat_v), (wuv_hbm, wuv), (wout_hbm, wout), (wg_hbm.at[0], wg), (wu_hbm.at[0], wu), (wd_hbm.at[0], wd)]
        )
    ]
    for cp in loads:
        cp.start()
    barrier = pltpu.get_barrier_semaphore()

    @pl.loop(1, 8)
    def _(k):
        pl.semaphore_signal(barrier, inc=1, device_id=dp_to(k // 2, k % 2), device_id_type=MESH)

    @pl.loop(1, 32)
    def _(k):
        pl.semaphore_signal(barrier, inc=1, device_id=(i, ex_at(k // 8, k % 8)), device_id_type=MESH)

    loads[0].wait()

    low_lane = iota((64, 128), 1) < 64
    low16 = iota((16, 128), 1) < 64
    row16 = iota((16, 128), 0)

    @pl.loop(0, 8)
    def _(k):
        dest = ((x + k // 2) % 4) * 2 + (c + k % 2) % 2
        pages = [mv_ref[dest, m] for m in range(4)]
        for m in range(4):
            slat[k, m * 64 : (m + 1) * 64, :] = lat_v[pages[m]]
        for m in range(2):
            a = rope_ref[pages[2 * m]].astype(F32)
            b = rope_ref[pages[2 * m + 1]].astype(F32)
            srope[k, m * 64 : (m + 1) * 64, :] = jnp.where(low_lane, a, b).astype(BF16)
        scales = [ps_ref[pages[m]] for m in range(4)]
        first = jnp.where(low16, scales[0], scales[1])
        second = jnp.where(low16, scales[2], scales[3])
        srope[k, 128:144, :] = jnp.where(row16 == 0, first, second).astype(BF16)

    def page_copies(k):
        dev = dp_to(k // 2, k % 2)
        return (
            rcopy(slat.at[k], rlat.at[k], pg_s.at[0, k], pg_r.at[0, k], dev),
            rcopy(srope.at[k], rrope.at[k], pg_s.at[1, k], pg_r.at[1, k], dev),
        )

    pl.semaphore_wait(barrier, 38)

    @pl.loop(1, 8)
    def _(k):
        for cp in page_copies(k):
            cp.start()

    e32 = iota((32, 32), 1)
    sel = jnp.zeros((32, 32), F32)
    for kk in range(8):
        sel = jnp.where(rt_ref[:, kk : kk + 1] == e32, 1.0, sel)
    r32 = iota((32, 32), 0)
    earlier = jnp.where((r32 // 4 == e32 // 4) & (e32 % 4 < r32 % 4), 1.0, 0.0).astype(BF16)
    cum = dot(earlier, sel.astype(BF16))
    code = sel * (cum + 1.0)
    lane512 = iota((32, 512), 1)
    row512 = iota((32, 512), 0)
    spread = jnp.where(lane512 // 16 == row512, 1.0, 0.0).astype(BF16)
    codes = dot(code.astype(BF16), spread)
    want = ((lane512 // 8) % 2 + 1).astype(F32)
    qt = jnp.where((codes == want) & (row512 // 4 == lane512 % 8), 1.0, 0.0)
    qt_s[...] = qt
    q_s[...] = qt.T.astype(BF16)
    res_l[...] = jnp.zeros_like(res_l)
    gain_l[...] = jnp.zeros_like(gain_l)
    d_f[...] = jnp.zeros_like(d_f)
    for k in range(NK):
        res_l[4 * k : 4 * k + 4, :] = res_ref[:, k * CH : (k + 1) * CH].astype(F32)
        gain_l[4 * k : 4 * k + 4, :] = jnp.broadcast_to(gain_ref[:, k * CH : (k + 1) * CH], (4, CH))

    zeros64 = jnp.zeros((256, 64), F32)
    qr = qr_ref[...].astype(F32)
    q_l[...] = jnp.concatenate([qr, zeros64], axis=1).astype(BF16)
    q_r[...] = jnp.concatenate([zeros64, qr], axis=1).astype(BF16)
    newk[...] = jnp.zeros_like(newk)
    newr[...] = jnp.zeros_like(newr)
    newk[0:4, :] = nl_ref[...].astype(F32)
    newr[0:4, 0:64] = nr_ref[...].astype(F32)
    nk = newk[...].astype(BF16)
    s = (dot_nt(q_ref[...], nk) + dot_nt(q_l[...], newr[...].astype(BF16))) * SCORE_SCALE
    row = iota((256, 128), 0)
    col = iota((256, 128), 1)
    ok = (col < 4) & (col // 2 == row // 128) & (col % 2 <= (row // 64) % 2)
    s = jnp.where(ok, s, NEG)
    m = jnp.max(s, -1, keepdims=True)
    p = jnp.exp(s - m)
    m_s[...] = jnp.broadcast_to(m, (256, 128))
    l_s[...] = jnp.broadcast_to(jnp.sum(p, -1, keepdims=True), (256, 128))
    o_s[...] = dot(p.astype(BF16), nk)

    def attend(keys, s_rope, scale, bias0, bias1):
        s = (dot_nt(q_ref[...], keys) + s_rope) * (scale * SCORE_SCALE)
        s = jnp.concatenate([s[:128] + bias0, s[128:] + bias1], axis=0)
        m_old = m_s[:, 0:1]
        m_new = jnp.maximum(m_old, jnp.max(s, -1, keepdims=True))
        p = jnp.exp(s - m_new)
        alpha = jnp.exp(m_old - m_new)
        m_s[...] = jnp.broadcast_to(m_new, (256, 128))
        l_s[...] = jnp.broadcast_to(l_s[:, 0:1] * alpha + jnp.sum(p, -1, keepdims=True), (256, 128))
        o_s[...] = o_s[...] * alpha + dot((p * scale).astype(BF16), keys)

    @pl.loop(0, 12)
    def _(n):
        keys = lat_v[pl.ds(n * 4, 4)].reshape(256, 512)
        ropes = rope_ref[pl.ds(n * 4, 4)].reshape(256, 128)
        a = aux_ref[n]
        attend(keys, dot_nt(q_l[...], ropes), a[0:1], a[1:2], a[2:3])

    def attend_moved(k, lat_at, rope_at):
        source = ((x - k // 2 + 4) % 4) * 2 + (c + k % 2) % 2
        a = aux_ref[12 + source]
        ropes = rope_at[0:128, :]
        lo = dot_nt(q_l[...], ropes)
        hi = dot_nt(q_r[...], ropes)
        s_rope = jnp.concatenate([lo[:, :64], hi[:, :64], lo[:, 64:], hi[:, 64:]], axis=1)
        sc = rope_at[128:144, :].astype(F32)
        scale = jnp.concatenate([sc[0:1], sc[1:2]], axis=1)
        attend(lat_at[...], s_rope, scale, a[1:2], a[2:3])

    attend_moved(0, slat.at[0], srope.at[0])

    @pl.loop(1, 8)
    def _(k):
        for cp in page_copies(k):
            cp.wait_recv()
        attend_moved(k, rlat.at[k], rrope.at[k])

    loads[1].wait()
    loads[2].wait()

    o = (o_s[...] / l_s[:, 0:1]).astype(BF16)
    pr = iota((256, 256), 0)
    pc = iota((256, 256), 1)
    perm = jnp.where(pc == (pr // 2 % 4) * 64 + (pr // 8) * 2 + pr % 2, 1.0, 0.0).astype(BF16)
    oa = dot(perm, o[:, :256]).reshape(32, 8, 256)
    ob = dot(perm, o[:, 256:]).reshape(32, 8, 256)
    so[...] = jnp.concatenate([oa, ob], axis=1).astype(BF16)

    def o_copy(k):
        e = ex_at(k // 8, k % 8)
        return rcopy(so.at[e], ro.at[j], o_ss.at[k], o_rs.at[k], (i, e))

    @pl.loop(1, 32)
    def _(k):
        o_copy(k).start()

    ro[j] = so[j]

    @pl.loop(1, 32)
    def _(k):
        o_copy(k).wait_recv()

    got = ro[...].astype(F32)
    g0 = got[:, :8, :].reshape(256, 256).astype(BF16)
    g1 = got[:, 8:, :].reshape(256, 256).astype(BF16)
    wcat = jnp.concatenate([wuv[0], wuv[1]], axis=1)
    hv = dot(g0, wcat[:256]) + dot(g1, wcat[256:])
    hv = jnp.where(pr % 2 == pc // 128, hv, 0.0).astype(BF16)
    fold = jnp.where(iota((128, 256), 0) == iota((128, 256), 1) // 2, 1.0, 0.0).astype(BF16)
    hv_s[...] = dot(fold, hv).astype(BF16)

    for k in range(NK):
        w = slice(k * CH, (k + 1) * CH)
        part = dot(hv_s[...], wout[:, w]).reshape(4, 32, CH)
        pf[:, :, w] = part
        ps1[:, :, w] = part.astype(BF16)

    def y_copy(n):
        yy = (y + n) % 4
        return rcopy(ps1.at[yy], pr1.at[n], p1_s.at[n], p1_r.at[n], (i, ex_at(n, 0)))

    for n in (1, 3, 2):
        y_copy(n).start()
    for n in (1, 3, 2):
        y_copy(n).wait_recv()
    s_f[...] = pf[y] + pr1[1].astype(F32) + pr1[2].astype(F32) + pr1[3].astype(F32)
    for zz in range(8):
        for k in range(NK):
            d_f[zz, 4 * k : 4 * k + 4, :] = s_f[4 * zz : 4 * zz + 4, k * CH : (k + 1) * CH]
    sp2[...] = d_f[...].astype(BF16)

    def z_copy(n):
        zz = (z + n) % 8
        return rcopy(sp2.at[zz], pr2.at[n], p2_s.at[n], p2_r.at[n], (i, ex_at(0, n)))

    for n in (4, 3, 5, 2, 6, 1, 7):
        z_copy(n).start()
    total = d_f[z]
    for n in range(1, 8):
        z_copy(n).wait_recv()
        total = total + pr2[n].astype(F32)
    al_f[...] = total

    hidden = (res_l[...] + total).astype(BF16).astype(F32)
    same = jnp.where(r32 % 4 == e32 % 4, 1.0, 0.0)
    sq = jnp.broadcast_to(jnp.sum(hidden * hidden, -1, keepdims=True), (32, 128))
    sq = jnp.dot(same, sq, precision=lax.Precision.HIGHEST, preferred_element_type=F32)
    normed = (hidden * lax.rsqrt(sq[:, 0:1] / D + NORM_EPS) * gain_l[...]).astype(BF16)
    sd[...] = dot(q_s[...], normed).astype(BF16).reshape(32, 16, CH)

    def d_copy(k):
        e = ex_at(k // 8, k % 8)
        return rcopy(sd.at[e], rd.at[k], d_ss.at[k], d_rs.at[k], (i, e))

    @pl.loop(1, 32)
    def _(k):
        d_copy(k).start()

    rd[0] = sd[j]

    acc = jnp.zeros((32, 32), F32)
    for k in range(NK):
        lg = dot_nt(normed, wr_ref[:, k * CH : (k + 1) * CH])
        acc = acc + jnp.where(r32 // 4 == k, lg, 0.0)
    logits = jnp.dot(same, acc, precision=lax.Precision.HIGHEST, preferred_element_type=F32)
    sig = sel / (1.0 + jnp.exp(-logits))
    gates = ROUTE_SCALE * sig / jnp.sum(sig, -1, keepdims=True)
    g_hi = gates.astype(BF16)
    g_lo = (gates - g_hi.astype(F32)).astype(BF16)
    c_hi = (dot(g_hi, spread) * qt_s[...]).astype(BF16)
    c_lo = (dot(g_lo, spread) * qt_s[...]).astype(BF16)
    for k in range(NK):
        attn_ref[:, k * CH : (k + 1) * CH] = al_f[4 * k : 4 * k + 4, :].astype(BF16)
    for n in range(3, 6):
        loads[n].wait()

    def ag(g, n):
        lo, hi = pl.ds(0, HALF), pl.ds(HALF, HALF)
        src, dst, dev = [
            (xr.at[g, 0], xr.at[g, 3], right),
            (xr.at[g, 0], xr.at[g, 1], left),
            (xr.at[g, 3, :, lo], xr.at[g, 2, :, lo], right),
            (xr.at[g, 1, :, hi], xr.at[g, 2, :, hi], left),
            (xr.at[g, 0], xr.at[g, 4], sib),
            (xr.at[g, 3], xr.at[g, 7], sib),
            (xr.at[g, 1], xr.at[g, 5], sib),
            (xr.at[g, 2], xr.at[g, 6], sib),
        ][n]
        return rcopy(src, dst, ag_s.at[g, n], ag_r.at[g, n], dev)

    def rs(g, n):
        lo, hi = pl.ds(0, HALF), pl.ds(HALF, HALF)
        src, dst, dev = [
            (pp.at[g, pl.ds(4, 4)], sr.at[g], sib),
            (hb.at[g, :, lo], hr.at[g, 0], right),
            (hb.at[g, :, hi], hr.at[g, 1], left),
            (fb.at[g, 0], fr.at[g, 0], right),
            (fb.at[g, 1], fr.at[g, 1], left),
        ][n]
        return rcopy(src, dst, rs_s.at[g, n], rs_r.at[g, n], dev)

    def b_copy(k):
        e = ex_at(-(k // 8), -(k % 8))
        return rcopy(sret.at[k], rret.at[j], b_ss.at[k], b_rs.at[k], (i, e))

    def stage_a(g):
        @pl.loop(0, 8)
        def _(n):
            @pl.when(g * 8 + n > 0)
            def _():
                d_copy(g * 8 + n).wait_recv()

        got = rd[pl.ds(g * 8, 8)].reshape(128, CH).astype(F32)
        for b in range(4):
            t_f[b * 128 : (b + 1) * 128, :] = got[:, b * 128 : (b + 1) * 128]
        for k in range(NK):
            for b in range(4):
                at = k * CH + b * 128
                xr[g, 0, :, at : at + 128] = t_f[pl.ds(b * 128 + k, 16, stride=8), :].astype(BF16)
        for n in (0, 1, 4):
            ag(g, n).start()

    def stage_b(g):
        ag(g, 0).wait_recv()
        ag(g, 2).start()
        ag(g, 5).start()
        ag(g, 1).wait_recv()
        ag(g, 3).start()
        ag(g, 6).start()

    def stage_c(g):
        ag(g, 2).wait_recv()
        ag(g, 3).wait_recv()
        ag(g, 7).start()
        for n in range(4, 8):
            ag(g, n).wait_recv()

    def stage_d(g):
        rows = xr[g].reshape(128, D)
        gate = dot(rows, wg[...])
        up = dot(rows, wu[...])
        h = (gate / (1.0 + jnp.exp(-gate)) * up).astype(BF16)
        for k in range(NK):
            w = slice(k * CH, (k + 1) * CH)
            pp[g, :, :, w] = dot(h, wd[:, w]).astype(BF16).reshape(8, 16, CH)
        rs(g, 0).start()

    def stage_e(g):
        rs(g, 0).wait_recv()
        ss[g] = pp[g, 0:4].astype(F32) + sr[g].astype(F32)
        hb[g] = ss[g, 2].astype(BF16)
        rs(g, 1).start()
        rs(g, 2).start()

    def stage_f(g):
        rs(g, 1).wait_recv()
        fb[g, 0, :, 0:HALF] = (ss[g, 1, :, 0:HALF] + hr[g, 0].astype(F32)).astype(BF16)
        fb[g, 0, :, HALF:] = ss[g, 1, :, HALF:].astype(BF16)
        rs(g, 3).start()
        rs(g, 2).wait_recv()
        fb[g, 1, :, 0:HALF] = ss[g, 3, :, 0:HALF].astype(BF16)
        fb[g, 1, :, HALF:] = (ss[g, 3, :, HALF:] + hr[g, 1].astype(F32)).astype(BF16)
        rs(g, 4).start()

    def stage_g(g):
        rs(g, 3).wait_recv()
        rs(g, 4).wait_recv()
        for b in range(4):
            for k in range(NK):
                w = slice(k * CH + b * 128, k * CH + b * 128 + 128)
                v = ss[g, 0, :, w] + fr[g, 0, :, w].astype(F32) + fr[g, 1, :, w].astype(F32)
                t_f[pl.ds(b * 128 + k, 16, stride=8), :] = v
            t_f[pl.ds(b * 128 + 7, 16, stride=8), :] = jnp.zeros((16, 128), F32)
        back = jnp.concatenate([t_f[b * 128 : (b + 1) * 128, :] for b in range(4)], axis=1)
        sret[pl.ds(g * 8, 8)] = back.astype(BF16).reshape(8, 16, CH)

        @pl.loop(0, 8)
        def _(n):
            @pl.when(g * 8 + n > 0)
            def _():
                b_copy(g * 8 + n).start()

    stages = [(stage_a, 0), (stage_b, 1), (stage_c, 2), (stage_d, 2), (stage_e, 3), (stage_f, 4), (stage_g, 5)]

    @pl.loop(0, 9)
    def _(t):
        for fn, lag in stages:

            @pl.when((t >= lag) & (t < lag + 4))
            def _(fn=fn, lag=lag):
                fn(t - lag)

    rret[j] = sret[0]

    @pl.loop(1, 32)
    def _(k):
        b_copy(k).wait_recv()

    rows = rret[...].reshape(512, CH)
    al_f[...] = dot(c_hi, rows) + dot(c_lo, rows)
    for k in range(NK):
        moe_ref[:, k * CH : (k + 1) * CH] = al_f[4 * k : 4 * k + 4, :].astype(BF16)

    @pl.loop(1, 8)
    def _(k):
        for cp in page_copies(k):
            cp.wait_send()

    @pl.loop(1, 32)
    def _(k):
        o_copy(k).wait_send()
        d_copy(k).wait_send()
        b_copy(k).wait_send()

    for n in (1, 2, 3):
        y_copy(n).wait_send()
    for n in range(1, 8):
        z_copy(n).wait_send()

    @pl.loop(0, 4)
    def _(g):
        for n in range(8):
            ag(g, n).wait_send()
        for n in range(5):
            rs(g, n).wait_send()


def body(
    cache_lat, cache_rope, page_scale, move_list, page_table, lengths, q_lat, q_rope, new_lat, new_rope,
    w_uv, w_out, residual, norm_gain, w_router, routes, w_gate, w_up, w_down,
):
    slots, page = cache_lat.shape[0], cache_lat.shape[1]
    rope3 = cache_rope.reshape(slots, page, 64)
    rope2 = jnp.concatenate([rope3, rope3], axis=-1)
    ps = page_scale.astype(F32)
    names = page_table[:, :, None] == jnp.arange(80, dtype=jnp.int32)
    left_tokens = lengths[:, None] - jnp.arange(32, dtype=jnp.int32)[None, :] * page
    limit = jnp.max(jnp.where(names, left_tokens[:, :, None], 0), axis=1)
    bias = jnp.where(jnp.arange(page, dtype=jnp.int32) < limit[:, :, None], 0.0, NEG).reshape(2, 20, 256)
    token_scale = jnp.broadcast_to(jnp.pad(ps, (0, 32))[:, None], (80, page)).reshape(1, 20, 256)
    aux = jnp.concatenate([token_scale, bias, jnp.zeros((5, 20, 256), F32)], axis=0).transpose(1, 0, 2)
    routes32 = jnp.tile(routes, (8, 1))

    any_spec = pl.BlockSpec(memory_space=pl.ANY)
    vmem = pl.BlockSpec(memory_space=pltpu.VMEM)
    smem = pl.BlockSpec(memory_space=pltpu.SMEM)
    dma = pltpu.SemaphoreType.DMA
    vm = pltpu.VMEM
    attn, moe = pl.pallas_call(
        kernel,
        out_shape=[jax.ShapeDtypeStruct((4, D), BF16)] * 2,
        in_specs=[smem, smem, any_spec] + [vmem] * 6 + [any_spec] * 2 + [vmem] * 4 + [any_spec] * 3,
        out_specs=[vmem] * 2,
        scratch_shapes=[
            vm((48, 64, 512), BF16), vm((2, 512, 128), BF16), vm((256, D), BF16),
            vm((D, 256), BF16), vm((D, 256), BF16), vm((256, D), BF16),
            vm((8, 256, 512), BF16), vm((8, 144, 128), BF16), vm((8, 256, 512), BF16), vm((8, 144, 128), BF16),
            vm((128, 512), F32), vm((128, 128), F32), vm((256, 128), BF16), vm((256, 128), BF16),
            vm((256, 128), F32), vm((256, 128), F32), vm((256, 512), F32),
            vm((32, 16, 256), BF16), vm((32, 16, 256), BF16), vm((128, 256), BF16),
            vm((4, 32, D), F32), vm((4, 32, D), BF16), vm((4, 32, D), BF16), vm((32, D), F32),
            vm((8, 32, CH), F32), vm((8, 32, CH), BF16), vm((8, 32, CH), BF16),
            vm((32, CH), F32), vm((32, CH), F32), vm((32, CH), F32),
            vm((512, 32), BF16), vm((32, 512), F32), vm((32, 16, CH), BF16), vm((32, 16, CH), BF16),
            vm((512, 128), F32), vm((4, 8, 16, D), BF16), vm((4, 8, 16, D), BF16), vm((4, 4, 16, D), BF16),
            vm((4, 4, 16, D), F32), vm((4, 16, D), BF16), vm((4, 2, 16, HALF), BF16),
            vm((4, 2, 16, D), BF16), vm((4, 2, 16, D), BF16), vm((32, 16, CH), BF16), vm((32, 16, CH), BF16),
            dma((6,)), dma((2, 8)), dma((2, 8)), dma((32,)), dma((32,)), dma((4,)), dma((4,)),
            dma((8,)), dma((8,)), dma((32,)), dma((32,)), dma((4, 8)), dma((4, 8)), dma((4, 5)), dma((4, 5)),
            dma((32,)), dma((32,)),
        ],
        compiler_params=pltpu.CompilerParams(
            collective_id=0, has_side_effects=True, vmem_limit_bytes=60 * 2**20
        ),
        name="step",
    )(
        move_list[0], ps, cache_lat, rope2, aux, q_lat.reshape(256, 512), q_rope.reshape(256, 64),
        new_lat.reshape(4, 512), new_rope.reshape(4, 64), w_uv, w_out, residual, norm_gain.reshape(1, D),
        w_router.T, routes32, w_gate, w_up, w_down,
    )
    return attn, moe


def solution(mesh):
    both = ("dp", "expert")
    return jax.shard_map(
        body,
        mesh=mesh,
        in_specs=(
            P(both, None, None), P(both, None), P(both), P(both, None, None), P(both, None), P(both),
            P(both, None, None, None), P(both, None, None, None), P(both, None, None), P(both, None, None),
            P("expert", None, None), P("expert", None), P(both, None), P(), P(), P(both, None),
            P("expert", None, "dp"), P("expert", None, "dp"), P("expert", "dp", None),
        ),
        out_specs=(P(both, None), P(both, None)),
        check_vma=False,
    )
```

time: 484 us -> 140 us (0.29)
  waiting for transfers between devices: 334 us -> 0 us
  Pallas kernels: 0 us -> 128 us
  blocking collectives: 47.9 us -> 0 us
  starting transfers between devices: 25.6 us -> 0 us
  local copies, waits for them, and re-layouts: 32 us -> 7.65 us
  matrix products: 20.8 us -> 0 us
  between operations: 14.9 us -> 0.78 us
  other arithmetic: 8.38 us -> 2.86 us
    unnamed x5 -> x0, waiting for transfers between devices: 202 us -> none
    pallas_call x0 -> x1, Pallas kernels: none -> 128 us  [body(): pl.pallas_call(kernel, out_shape=[jax.ShapeDtypeStruct((4, D), BF16)] * 2...]
    all_to_all x4 -> x0, waiting for transfers between devices: 95.8 us -> none  [the longest x1 69.6 us: body(): lax.all_to_all(partial_out.astype(jnp.bfloat16), 'expert', split_axis=0,...]
    all_to_all x2 -> x0, blocking collectives: 36.1 us -> none  [the longest x1 20 us: body(): lax.all_to_all(latent_out, 'expert', split_axis=2, concat_axis=0, tiled=T...]
    all_gather x1 -> x0, waiting for transfers between devices: 36 us -> none  [body(): grouped = lax.all_gather(arrived, 'dp', axis=1, tiled=True)]
    all_to_all x4 -> x0, starting transfers between devices: 25.5 us -> none  [the longest x1 9.68 us: body(): lax.all_to_all(partial_out.astype(jnp.bfloat16), 'expert', split_axis=0,...]
    dot_general x14 -> x0, matrix products: 20.8 us -> none  [the longest x1 5.95 us: body(): jnp.einsum('ktec,ekcd->ktd', combine_weights, returned, precision=highest)]
    gather x7 -> x0, local copies, waits for them, and re-layouts: 13.9 us -> none  [the longest x4 6.9 us: body(): sent = (cache_lat[picked], cache_rope[picked], page_scale[picked])]
  transfers between devices with their start and end apart: 7 -> 0, of which waited for: 7 -> 0; matrix products, arithmetic and copies ran while one was open for 3% -> 0% of each run, Pallas kernels for 0% -> 0%
where the time goes in v1:
time: 140 us
  Pallas kernels  128 us (91%)
  local copies, waits for them, and re-layouts  7.65 us (5%)
  other arithmetic  2.86 us (2%)
    pallas_call x1, Pallas kernels, body(): pl.pallas_call(kernel, out_shape=[jax.ShapeDtypeStruct((4, D), BF16)] * 2...  128 us

profile of v1, /device:TPU:1, one launch (start us, length us, event | category | flops | bytes accessed | tf_op | source)
XLA Modules:
  0.0 139.5 jit_solution(15550701708051817722)
XLA Ops:
  0.6 0.0 copy-start.5
  0.6 0.0 copy-start.4
  0.7 1.8 %reshape.75 = bf16[48,64,64]{2,1,0:T(8,128)(2,1)S(1)} reshape(bf16[48,4096]{1,0:T(8,128)(2,1)} %param.20) | data formatting | bytes 786432 | tf_op jit(solution)/shard_map/reshape | solution.py:448
  2.5 1.3 pad_maximum_fusion.rope_ref
  3.9 0.1 broadcast_subtract_fusion
  3.9 0.1 select_reduce_fusion
  4.0 0.1 lt.23
  4.1 0.1 lt.24
  4.2 0.1 lt.21
  4.3 0.1 broadcast_in_dim.40
  4.4 0.1 broadcast_in_dim.41
  4.5 0.1 broadcast_in_dim.42
  4.6 0.1 pad.7.clone
  4.7 0.8 maximum_bitcast_fusion.aux_ref
  5.5 0.6 tile.4
  6.1 0.0 copy-done
  6.1 0.6 reshape.80.gain_ref
  6.7 0.0 copy-done.3
  6.7 0.7 copy.25.mv_ref
  7.4 0.6 reshape.78.nl_ref
  8.0 0.6 convert_element_type.5.ps_ref
  8.5 128.2 %step.1 = (bf16[4,3584]{1,0:T(4,128)(2,1)}, bf16[4,3584]{1,0:T(4,128)(2,1)}) custom-call(s32[8,4]{1,0:T(8,128)} %copy.25.mv_ref, f32[48]{0:T(128)} %convert_element_type.5.ps_ref, bf16[48,64,512]{2,1,0:T(8,128)(2,1)} %lat_hbm.1, bf16[48,64,128]{2,1,0:T(8,128)(2,1)} %pad_maximum_fusion.rope_ref, f32[20,8,256]{2,1,0:T(8,128)} %maximum_bitcast_fusion.aux_ref, ...), custom_call_target="tpu_custom_call" | custom-call | tf_op jit(solution)/shard_map/step/pallas_call | solution.py:464
  136.8 1.4 copy.29
  138.2 1.4 copy.30
  (15 shorter events, 0.1 us)
Async XLA Ops:
  0.6 3.2 %copy-start.5 = (s32[2]{0:T(128)S(1)}, s32[2]{0:T(128)}, u32[]{:S(2)}) copy-start(s32[2]{0:T(128)} %param.24) | copy-start | bytes 28
  0.6 3.3 %copy-start.4 = (s32[2,32]{1,0:T(2,128)S(1)}, s32[2,32]{1,0:T(2,128)}, u32[]{:S(2)}) copy-start(s32[2,32]{1,0:T(2,128)} %param.23) | copy-start | bytes 772
  0.7 3.7 %copy-start.6 = (bf16[48]{0:T(256)(128)(2,1)S(1)}, bf16[48]{0:T(256)(128)(2,1)}, u32[]{:S(2)}) copy-start(bf16[48]{0:T(256)(128)(2,1)} %param.21) | copy-start | bytes 292
  0.7 4.8 %copy-start.2 = (s32[4,8]{1,0:T(4,128)S(1)}, s32[4,8]{1,0:T(4,128)}, u32[]{:S(2)}) copy-start(s32[4,8]{1,0:T(4,128)} %param.34) | copy-start | bytes 388
  0.7 5.4 %copy-start = (f32[3584]{0:T(1024)S(1)}, f32[3584]{0:T(1024)}, u32[]{:S(2)}) copy-start(f32[3584]{0:T(1024)} %param.32) | copy-start | bytes 43012
  0.7 6.0 %copy-start.3 = (s32[1,8,4]{1,2,0:T(4,128)S(1)}, s32[1,8,4]{1,2,0:T(4,128)}, u32[]{:S(2)}) copy-start(s32[1,8,4]{1,2,0:T(4,128)} %param.22) | copy-start | bytes 388
  0.7 6.7 %copy-start.1 = (bf16[2,2,512]{2,1,0:T(2,128)(2,1)S(1)}, bf16[2,2,512]{2,1,0:T(2,128)(2,1)}, u32[]{:S(2)}) copy-start(bf16[2,2,512]{2,1,0:T(2,128)(2,1)} %param.27) | copy-start | bytes 12292

commit v2 on v1

--- a/solution.py
+++ b/solution.py
@@ -31,14 +31,16 @@
 
 
 def kernel(
-    mv_ref, ps_ref, lat_hbm, rope_ref, aux_ref, q_ref, qr_ref, nl_ref, nr_ref,
-    wuv_hbm, wout_hbm, res_ref, gain_ref, wr_ref, rt_ref, wg_hbm, wu_hbm, wd_hbm,
-    attn_ref, moe_ref,
+    mv_hbm, ps_hbm, len_hbm, pt_hbm, lat_hbm, rope_hbm, q_hbm, qr_hbm, nl_hbm, nr_hbm,
+    wuv_hbm, wout_hbm, res_hbm, gain_hbm, wr_hbm, rt_hbm, wg_hbm, wu_hbm, wd_hbm,
+    out_ref,
+    mv_ref, ps_ref, len_ref, pt_ref, rope_raw, q_ref, qr_ref, nl_ref, nr_ref, res_ref, gain_ref, wr_ref, rt_ref,
+    rope_f, rope_ref, bias_s, scale_s, rt_s,
     lat_v, wuv, wout, wg, wu, wd,
     slat, srope, rlat, rrope, newk, newr, q_l, q_r, m_s, l_s, o_s,
-    so, ro, hv_s, pf, ps1, pr1, s_f, d_f, sp2, pr2, al_f, res_l, gain_l,
+    so, ro, s_f, d_f, sp2, pr2, al_f, res_l, gain_l,
     q_s, qt_s, sd, rd, t_f, xr, pp, sr, ss, hb, hr, fb, fr, sret, rret,
-    lsem, pg_s, pg_r, o_ss, o_rs, p1_s, p1_r, p2_s, p2_r, d_ss, d_rs, ag_s, ag_r, rs_s, rs_r, b_ss, b_rs,
+    lsem, pg_s, pg_r, w_ss, w_rs, o_ss, o_rs, p2_s, p2_r, d_ss, d_rs, ag_s, ag_r, rs_s, rs_r, b_ss, b_rs,
 ):
     i = lax.axis_index("dp")
     j = lax.axis_index("expert")
@@ -56,26 +58,98 @@
         )
 
     right, left, sib = dp_to(1, 0), dp_to(3, 0), dp_to(0, 1)
-
-    loads = [
-        pltpu.make_async_copy(a, b, lsem.at[n])
-        for n, (a, b) in enumerate(
-            [(lat_hbm, lat_v), (wuv_hbm, wuv), (wout_hbm, wout), (wg_hbm.at[0], wg), (wu_hbm.at[0], wu), (wd_hbm.at[0], wd)]
-        )
+    barrier = pltpu.get_barrier_semaphore()
+
+    @pl.loop(1, 8)
+    def _(k):
+        pl.semaphore_signal(barrier, inc=1, device_id=dp_to(k // 2, k % 2), device_id_type=MESH)
+
+    pairs = [
+        (mv_hbm.at[0], mv_ref), (ps_hbm, ps_ref), (lat_hbm, lat_v), (rope_hbm, rope_raw), (wuv_hbm, wuv.at[0]),
+        (wout_hbm, wout.at[0]), (len_hbm, len_ref), (pt_hbm, pt_ref), (q_hbm, q_ref), (qr_hbm, qr_ref),
+        (nl_hbm, nl_ref), (nr_hbm, nr_ref), (rt_hbm, rt_ref), (res_hbm, res_ref), (gain_hbm, gain_ref),
+        (wr_hbm, wr_ref), (wg_hbm.at[0], wg), (wu_hbm.at[0], wu), (wd_hbm.at[0], wd),
     ]
+    loads = [pltpu.make_async_copy(a, b, lsem.at[n]) for n, (a, b) in enumerate(pairs)]
     for cp in loads:
         cp.start()
-    barrier = pltpu.get_barrier_semaphore()
+
+    @pl.loop(1, 32)
+    def _(k):
+        pl.semaphore_signal(barrier, inc=1, device_id=(i, ex_at(k // 8, k % 8)), device_id_type=MESH)
+
+    for n in range(3):
+        loads[n].wait()
+
+    def dest_of(k):
+        return ((x + k // 2) % 4) * 2 + (c + k % 2) % 2
+
+    @pl.loop(0, 8)
+    def _(k):
+        dest = dest_of(k)
+        for m in range(4):
+            slat[k, m * 64 : (m + 1) * 64, :] = lat_v[mv_ref[m, dest]]
+
+    def page_copy(k, n):
+        dev = dp_to(k // 2, k % 2)
+        if n == 0:
+            return rcopy(slat.at[k], rlat.at[k], pg_s.at[0, k], pg_r.at[0, k], dev)
+        return rcopy(srope.at[k], rrope.at[k], pg_s.at[1, k], pg_r.at[1, k], dev)
+
+    up_y, down_y = (i, ex_at(1, 0)), (i, ex_at(-1, 0))
+
+    def w_copy(kind, n):
+        if kind == 0:
+            own = [wuv.at[d, c] for d in range(4)]
+            up = [wuv.at[d, c, pl.ds(0, 256)] for d in range(4)]
+            down = [wuv.at[d, c, pl.ds(256, 256)] for d in range(4)]
+            near_up = near_down = own
+        else:
+            rows = pl.ds(c * 128, 128)
+            own = [wout.at[d, rows] for d in range(4)]
+            up = [wout.at[d, rows, pl.ds(0, HALF)] for d in range(4)]
+            down = [wout.at[d, rows, pl.ds(HALF, HALF)] for d in range(4)]
+            near_up, near_down = (up, down) if kind == 1 else (down, up)
+        src, dst, dev = [
+            (near_up[0], near_up[3], up_y),
+            (near_down[0], near_down[1], down_y),
+            (up[3], up[2], up_y),
+            (down[1], down[2], down_y),
+            (near_up[3], near_up[3], sib),
+            (near_down[1], near_down[1], sib),
+            (own[2], own[2], sib),
+        ][n]
+        return rcopy(src, dst, w_ss.at[kind, n], w_rs.at[kind, n], dev)
+
+    pl.semaphore_wait(barrier, 38)
 
     @pl.loop(1, 8)
     def _(k):
-        pl.semaphore_signal(barrier, inc=1, device_id=dp_to(k // 2, k % 2), device_id_type=MESH)
-
-    @pl.loop(1, 32)
-    def _(k):
-        pl.semaphore_signal(barrier, inc=1, device_id=(i, ex_at(k // 8, k % 8)), device_id_type=MESH)
-
-    loads[0].wait()
+        page_copy(k, 0).start()
+
+    loads[4].wait()
+    loads[5].wait()
+    for kind in range(3):
+        w_copy(kind, 0).start()
+        w_copy(kind, 1).start()
+
+    loads[3].wait()
+    low48 = iota((48, 128), 1) < 64
+    for g in range(32):
+        v = rope_raw[:, g * 128 : (g + 1) * 128].astype(F32)
+        w = pltpu.roll(v, 64, axis=1)
+        rope_f[pl.ds(2 * g, 48, stride=64), :] = jnp.where(low48, v, w)
+        rope_f[pl.ds(2 * g + 1, 48, stride=64), :] = jnp.where(low48, w, v)
+
+    @pl.loop(0, 48)
+    def _(n):
+        rope_ref[n] = rope_f[pl.ds(pl.multiple_of(n * 64, 64), 64), :].astype(BF16)
+
+    scales = jnp.concatenate([ps_ref[...].astype(F32).reshape(1, 48), jnp.zeros((1, 80), F32)], axis=1)
+    scale_s[...] = jnp.broadcast_to(scales, (128, 128)).T
+
+    def scale_of(v):
+        return scale_s[pl.ds(v, 1), :]
 
     low_lane = iota((64, 128), 1) < 64
     low16 = iota((16, 128), 1) < 64
@@ -83,37 +157,42 @@
 
     @pl.loop(0, 8)
     def _(k):
-        dest = ((x + k // 2) % 4) * 2 + (c + k % 2) % 2
-        pages = [mv_ref[dest, m] for m in range(4)]
-        for m in range(4):
-            slat[k, m * 64 : (m + 1) * 64, :] = lat_v[pages[m]]
+        dest = dest_of(k)
+        pages = [mv_ref[m, dest] for m in range(4)]
         for m in range(2):
             a = rope_ref[pages[2 * m]].astype(F32)
             b = rope_ref[pages[2 * m + 1]].astype(F32)
             srope[k, m * 64 : (m + 1) * 64, :] = jnp.where(low_lane, a, b).astype(BF16)
-        scales = [ps_ref[pages[m]] for m in range(4)]
+        scales = [scale_of(pages[m]) for m in range(4)]
         first = jnp.where(low16, scales[0], scales[1])
         second = jnp.where(low16, scales[2], scales[3])
         srope[k, 128:144, :] = jnp.where(row16 == 0, first, second).astype(BF16)
 
-    def page_copies(k):
-        dev = dp_to(k // 2, k % 2)
-        return (
-            rcopy(slat.at[k], rlat.at[k], pg_s.at[0, k], pg_r.at[0, k], dev),
-            rcopy(srope.at[k], rrope.at[k], pg_s.at[1, k], pg_r.at[1, k], dev),
-        )
-
-    pl.semaphore_wait(barrier, 38)
-
     @pl.loop(1, 8)
     def _(k):
-        for cp in page_copies(k):
-            cp.start()
-
+        page_copy(k, 1).start()
+
+    for n in range(6, 16):
+        loads[n].wait()
+    page_id = iota((80, 32), 0)
+    entry = iota((80, 32), 1)
+    in_page = iota((80, 128), 1) % 64
+    for r in range(2):
+        fits = jnp.where(pt_ref[r : r + 1, :] == page_id, len_ref[r] - entry * 64, 0)
+        limit = jnp.max(fits, axis=1, keepdims=True)
+        bias_s[r] = jnp.where(in_page < limit, 0.0, NEG)
+    low1 = iota((1, 128), 1) < 64
+
+    def bias_of(r, v):
+        b = [bias_s[r, pl.ds(v + m, 1), :] for m in range(4)]
+        return jnp.concatenate([jnp.where(low1, b[0], b[1]), jnp.where(low1, b[2], b[3])], axis=1)
+
+    for k in range(8):
+        rt_s[4 * k : 4 * k + 4, :] = rt_ref[...]
     e32 = iota((32, 32), 1)
     sel = jnp.zeros((32, 32), F32)
     for kk in range(8):
-        sel = jnp.where(rt_ref[:, kk : kk + 1] == e32, 1.0, sel)
+        sel = jnp.where(rt_s[:, kk : kk + 1] == e32, 1.0, sel)
     r32 = iota((32, 32), 0)
     earlier = jnp.where((r32 // 4 == e32 // 4) & (e32 % 4 < r32 % 4), 1.0, 0.0).astype(BF16)
     cum = dot(earlier, sel.astype(BF16))
@@ -131,7 +210,7 @@
     d_f[...] = jnp.zeros_like(d_f)
     for k in range(NK):
         res_l[4 * k : 4 * k + 4, :] = res_ref[:, k * CH : (k + 1) * CH].astype(F32)
-        gain_l[4 * k : 4 * k + 4, :] = jnp.broadcast_to(gain_ref[:, k * CH : (k + 1) * CH], (4, CH))
+        gain_l[4 * k : 4 * k + 4, :] = jnp.broadcast_to(gain_ref[k * CH : (k + 1) * CH].reshape(1, CH), (4, CH))
 
     zeros64 = jnp.zeros((256, 64), F32)
     qr = qr_ref[...].astype(F32)
@@ -139,8 +218,9 @@
     q_r[...] = jnp.concatenate([zeros64, qr], axis=1).astype(BF16)
     newk[...] = jnp.zeros_like(newk)
     newr[...] = jnp.zeros_like(newr)
-    newk[0:4, :] = nl_ref[...].astype(F32)
-    newr[0:4, 0:64] = nr_ref[...].astype(F32)
+    for r in range(2):
+        newk[2 * r : 2 * r + 2, :] = nl_ref[r].astype(F32)
+        newr[2 * r : 2 * r + 2, 0:64] = nr_ref[r].astype(F32)
     nk = newk[...].astype(BF16)
     s = (dot_nt(q_ref[...], nk) + dot_nt(q_l[...], newr[...].astype(BF16))) * SCORE_SCALE
     row = iota((256, 128), 0)
@@ -168,77 +248,86 @@
     def _(n):
         keys = lat_v[pl.ds(n * 4, 4)].reshape(256, 512)
         ropes = rope_ref[pl.ds(n * 4, 4)].reshape(256, 128)
-        a = aux_ref[n]
-        attend(keys, dot_nt(q_l[...], ropes), a[0:1], a[1:2], a[2:3])
+        sc = [scale_of(n * 4 + m) for m in range(4)]
+        scale = jnp.concatenate([jnp.where(low1, sc[0], sc[1]), jnp.where(low1, sc[2], sc[3])], axis=1)
+        attend(keys, dot_nt(q_l[...], ropes), scale, bias_of(0, n * 4), bias_of(1, n * 4))
 
     def attend_moved(k, lat_at, rope_at):
         source = ((x - k // 2 + 4) % 4) * 2 + (c + k % 2) % 2
-        a = aux_ref[12 + source]
+        v = 48 + source * 4
         ropes = rope_at[0:128, :]
         lo = dot_nt(q_l[...], ropes)
         hi = dot_nt(q_r[...], ropes)
         s_rope = jnp.concatenate([lo[:, :64], hi[:, :64], lo[:, 64:], hi[:, 64:]], axis=1)
         sc = rope_at[128:144, :].astype(F32)
         scale = jnp.concatenate([sc[0:1], sc[1:2]], axis=1)
-        attend(lat_at[...], s_rope, scale, a[1:2], a[2:3])
+        attend(lat_at[...], s_rope, scale, bias_of(0, v), bias_of(1, v))
 
     attend_moved(0, slat.at[0], srope.at[0])
 
-    @pl.loop(1, 8)
-    def _(k):
-        for cp in page_copies(k):
-            cp.wait_recv()
+    def moved_from(k):
+        page_copy(k, 0).wait_recv()
+        page_copy(k, 1).wait_recv()
         attend_moved(k, rlat.at[k], rrope.at[k])
 
-    loads[1].wait()
-    loads[2].wait()
+    def pass_on(kind):
+        w_copy(kind, 0).wait_recv()
+        if kind < 2:
+            w_copy(kind, 2).start()
+        w_copy(kind, 4).start()
+        w_copy(kind, 1).wait_recv()
+        if kind < 2:
+            w_copy(kind, 3).start()
+        w_copy(kind, 5).start()
+
+    pass_on(0)
+    moved_from(1)
+    pass_on(1)
+
+    @pl.loop(2, 4)
+    def _(k):
+        moved_from(k)
+
+    pass_on(2)
+
+    @pl.loop(4, 8)
+    def _(k):
+        moved_from(k)
 
     o = (o_s[...] / l_s[:, 0:1]).astype(BF16)
     pr = iota((256, 256), 0)
     pc = iota((256, 256), 1)
-    perm = jnp.where(pc == (pr // 2 % 4) * 64 + (pr // 8) * 2 + pr % 2, 1.0, 0.0).astype(BF16)
-    oa = dot(perm, o[:, :256]).reshape(32, 8, 256)
-    ob = dot(perm, o[:, 256:]).reshape(32, 8, 256)
-    so[...] = jnp.concatenate([oa, ob], axis=1).astype(BF16)
-
-    def o_copy(k):
-        e = ex_at(k // 8, k % 8)
-        return rcopy(so.at[e], ro.at[j], o_ss.at[k], o_rs.at[k], (i, e))
-
-    @pl.loop(1, 32)
-    def _(k):
-        o_copy(k).start()
-
-    ro[j] = so[j]
-
-    @pl.loop(1, 32)
-    def _(k):
-        o_copy(k).wait_recv()
-
-    got = ro[...].astype(F32)
-    g0 = got[:, :8, :].reshape(256, 256).astype(BF16)
-    g1 = got[:, 8:, :].reshape(256, 256).astype(BF16)
-    wcat = jnp.concatenate([wuv[0], wuv[1]], axis=1)
-    hv = dot(g0, wcat[:256]) + dot(g1, wcat[256:])
-    hv = jnp.where(pr % 2 == pc // 128, hv, 0.0).astype(BF16)
-    fold = jnp.where(iota((128, 256), 0) == iota((128, 256), 1) // 2, 1.0, 0.0).astype(BF16)
-    hv_s[...] = dot(fold, hv).astype(BF16)
-
+    source = (pr // 8 % 4) * 64 + ((y + pr // 2 % 4) % 4) * 16 + (pr // 32) * 2 + pr % 2
+    perm = jnp.where(pc == source, 1.0, 0.0).astype(BF16)
+    so[...] = dot(perm, o).astype(BF16).reshape(8, 32, CH)
+
+    def o_copy(n):
+        return rcopy(so.at[(z + n) % 8], ro.at[n], o_ss.at[n], o_rs.at[n], (i, ex_at(0, n)))
+
+    for n in (4, 3, 5, 2, 6, 1, 7):
+        o_copy(n).start()
+    ro[0] = so[z]
+    for kind in range(2):
+        w_copy(kind, 2).wait_recv()
+        w_copy(kind, 3).wait_recv()
+        w_copy(kind, 6).start()
+    for n in range(1, 8):
+        o_copy(n).wait_recv()
+
+    for n in (4, 5, 6):
+        w_copy(0, n).wait_recv()
+
+    wcat = jnp.concatenate([wuv[d, h] for d in range(4) for h in range(2)], axis=1)
+    hv = dot(ro[...].reshape(256, CH), wcat)
+    hv = jnp.where(iota((256, 1024), 0) % 8 == iota((256, 1024), 1) // 128, hv, 0.0).astype(BF16)
+    fr_, fc = iota((32, 256), 0), iota((32, 256), 1)
+    fold = jnp.where(fc // 8 == ((z - fr_ // 4 + 8) % 8) * 4 + fr_ % 4, 1.0, 0.0).astype(BF16)
+    hv = dot(fold, hv).astype(BF16)
+    for kind, n in ((1, 4), (1, 5), (1, 6), (2, 4), (2, 5)):
+        w_copy(kind, n).wait_recv()
     for k in range(NK):
         w = slice(k * CH, (k + 1) * CH)
-        part = dot(hv_s[...], wout[:, w]).reshape(4, 32, CH)
-        pf[:, :, w] = part
-        ps1[:, :, w] = part.astype(BF16)
-
-    def y_copy(n):
-        yy = (y + n) % 4
-        return rcopy(ps1.at[yy], pr1.at[n], p1_s.at[n], p1_r.at[n], (i, ex_at(n, 0)))
-
-    for n in (1, 3, 2):
-        y_copy(n).start()
-    for n in (1, 3, 2):
-        y_copy(n).wait_recv()
-    s_f[...] = pf[y] + pr1[1].astype(F32) + pr1[2].astype(F32) + pr1[3].astype(F32)
+        s_f[:, w] = sum(dot(hv[:, d * 256 : (d + 1) * 256], wout[d, :, w]) for d in range(4))
     for zz in range(8):
         for k in range(NK):
             d_f[zz, 4 * k : 4 * k + 4, :] = s_f[4 * zz : 4 * zz + 4, k * CH : (k + 1) * CH]
@@ -285,8 +374,8 @@
     c_hi = (dot(g_hi, spread) * qt_s[...]).astype(BF16)
     c_lo = (dot(g_lo, spread) * qt_s[...]).astype(BF16)
     for k in range(NK):
-        attn_ref[:, k * CH : (k + 1) * CH] = al_f[4 * k : 4 * k + 4, :].astype(BF16)
-    for n in range(3, 6):
+        out_ref[0:4, k * CH : (k + 1) * CH] = al_f[4 * k : 4 * k + 4, :].astype(BF16)
+    for n in range(16, 19):
         loads[n].wait()
 
     def ag(g, n):
@@ -414,22 +503,24 @@
     rows = rret[...].reshape(512, CH)
     al_f[...] = dot(c_hi, rows) + dot(c_lo, rows)
     for k in range(NK):
-        moe_ref[:, k * CH : (k + 1) * CH] = al_f[4 * k : 4 * k + 4, :].astype(BF16)
+        out_ref[4:8, k * CH : (k + 1) * CH] = al_f[4 * k : 4 * k + 4, :].astype(BF16)
 
     @pl.loop(1, 8)
     def _(k):
-        for cp in page_copies(k):
-            cp.wait_send()
+        page_copy(k, 0).wait_send()
+        page_copy(k, 1).wait_send()
 
     @pl.loop(1, 32)
     def _(k):
-        o_copy(k).wait_send()
         d_copy(k).wait_send()
         b_copy(k).wait_send()
 
-    for n in (1, 2, 3):
-        y_copy(n).wait_send()
+    for kind in range(3):
+        for n in range(7):
+            if kind < 2 or n in (0, 1, 4, 5):
+                w_copy(kind, n).wait_send()
     for n in range(1, 8):
+        o_copy(n).wait_send()
         z_copy(n).wait_send()
 
     @pl.loop(0, 4)
@@ -444,43 +535,38 @@
     cache_lat, cache_rope, page_scale, move_list, page_table, lengths, q_lat, q_rope, new_lat, new_rope,
     w_uv, w_out, residual, norm_gain, w_router, routes, w_gate, w_up, w_down,
 ):
-    slots, page = cache_lat.shape[0], cache_lat.shape[1]
-    rope3 = cache_rope.reshape(slots, page, 64)
-    rope2 = jnp.concatenate([rope3, rope3], axis=-1)
-    ps = page_scale.astype(F32)
-    names = page_table[:, :, None] == jnp.arange(80, dtype=jnp.int32)
-    left_tokens = lengths[:, None] - jnp.arange(32, dtype=jnp.int32)[None, :] * page
-    limit = jnp.max(jnp.where(names, left_tokens[:, :, None], 0), axis=1)
-    bias = jnp.where(jnp.arange(page, dtype=jnp.int32) < limit[:, :, None], 0.0, NEG).reshape(2, 20, 256)
-    token_scale = jnp.broadcast_to(jnp.pad(ps, (0, 32))[:, None], (80, page)).reshape(1, 20, 256)
-    aux = jnp.concatenate([token_scale, bias, jnp.zeros((5, 20, 256), F32)], axis=0).transpose(1, 0, 2)
-    routes32 = jnp.tile(routes, (8, 1))
-
     any_spec = pl.BlockSpec(memory_space=pl.ANY)
     vmem = pl.BlockSpec(memory_space=pltpu.VMEM)
-    smem = pl.BlockSpec(memory_space=pltpu.SMEM)
     dma = pltpu.SemaphoreType.DMA
     vm = pltpu.VMEM
-    attn, moe = pl.pallas_call(
+    operands = (
+        move_list.transpose(0, 2, 1), page_scale, lengths, page_table, cache_lat, cache_rope,
+        q_lat.reshape(256, 512), q_rope.reshape(256, 64), new_lat, new_rope, w_uv, w_out, residual,
+        norm_gain, w_router.T, routes, w_gate, w_up, w_down,
+    )
+    out = pl.pallas_call(
         kernel,
-        out_shape=[jax.ShapeDtypeStruct((4, D), BF16)] * 2,
-        in_specs=[smem, smem, any_spec] + [vmem] * 6 + [any_spec] * 2 + [vmem] * 4 + [any_spec] * 3,
-        out_specs=[vmem] * 2,
+        out_shape=jax.ShapeDtypeStruct((8, D), BF16),
+        in_specs=[any_spec] * len(operands),
+        out_specs=vmem,
         scratch_shapes=[
-            vm((48, 64, 512), BF16), vm((2, 512, 128), BF16), vm((256, D), BF16),
+            pltpu.SMEM((4, 8), jnp.int32), vm((48,), BF16), pltpu.SMEM((2,), jnp.int32), vm((2, 32), jnp.int32),
+            vm((48, 4096), BF16), vm((256, 512), BF16), vm((256, 64), BF16), vm((2, 2, 512), BF16), vm((2, 2, 64), BF16),
+            vm((4, D), BF16), vm((D,), F32), vm((32, D), BF16), vm((4, 8), jnp.int32),
+            vm((48 * 64, 128), F32), vm((48, 64, 128), BF16), vm((2, 80, 128), F32), vm((128, 128), F32), vm((32, 8), jnp.int32),
+            vm((48, 64, 512), BF16), vm((4, 2, 512, 128), BF16), vm((4, 256, D), BF16),
             vm((D, 256), BF16), vm((D, 256), BF16), vm((256, D), BF16),
             vm((8, 256, 512), BF16), vm((8, 144, 128), BF16), vm((8, 256, 512), BF16), vm((8, 144, 128), BF16),
             vm((128, 512), F32), vm((128, 128), F32), vm((256, 128), BF16), vm((256, 128), BF16),
             vm((256, 128), F32), vm((256, 128), F32), vm((256, 512), F32),
-            vm((32, 16, 256), BF16), vm((32, 16, 256), BF16), vm((128, 256), BF16),
-            vm((4, 32, D), F32), vm((4, 32, D), BF16), vm((4, 32, D), BF16), vm((32, D), F32),
+            vm((8, 32, CH), BF16), vm((8, 32, CH), BF16), vm((32, D), F32),
             vm((8, 32, CH), F32), vm((8, 32, CH), BF16), vm((8, 32, CH), BF16),
             vm((32, CH), F32), vm((32, CH), F32), vm((32, CH), F32),
             vm((512, 32), BF16), vm((32, 512), F32), vm((32, 16, CH), BF16), vm((32, 16, CH), BF16),
             vm((512, 128), F32), vm((4, 8, 16, D), BF16), vm((4, 8, 16, D), BF16), vm((4, 4, 16, D), BF16),
             vm((4, 4, 16, D), F32), vm((4, 16, D), BF16), vm((4, 2, 16, HALF), BF16),
             vm((4, 2, 16, D), BF16), vm((4, 2, 16, D), BF16), vm((32, 16, CH), BF16), vm((32, 16, CH), BF16),
-            dma((6,)), dma((2, 8)), dma((2, 8)), dma((32,)), dma((32,)), dma((4,)), dma((4,)),
+            dma((19,)), dma((2, 8)), dma((2, 8)), dma((3, 7)), dma((3, 7)), dma((8,)), dma((8,)),
             dma((8,)), dma((8,)), dma((32,)), dma((32,)), dma((4, 8)), dma((4, 8)), dma((4, 5)), dma((4, 5)),
             dma((32,)), dma((32,)),
         ],
@@ -488,12 +574,8 @@
             collective_id=0, has_side_effects=True, vmem_limit_bytes=60 * 2**20
         ),
         name="step",
-    )(
-        move_list[0], ps, cache_lat, rope2, aux, q_lat.reshape(256, 512), q_rope.reshape(256, 64),
-        new_lat.reshape(4, 512), new_rope.reshape(4, 64), w_uv, w_out, residual, norm_gain.reshape(1, D),
-        w_router.T, routes32, w_gate, w_up, w_down,
-    )
-    return attn, moe
+    )(*operands)
+    return out[:4], out[4:]
 
 
 def solution(mesh):

time: 140 us -> 116 us (0.83)
  Pallas kernels: 128 us -> 113 us
  local copies, waits for them, and re-layouts: 7.65 us -> 1.54 us
  other arithmetic: 2.86 us -> 0 us
    pallas_call x1, Pallas kernels: 128 us -> 113 us  [body(): pl.pallas_call(kernel, out_shape=jax.ShapeDtypeStruct((8, D), BF16), in_s...]
    reshape x3 -> x0, local copies, waits for them, and re-layouts: 3.01 us -> none  [the longest x1 1.8 us: body(): rope3 = cache_rope.reshape(slots, page, 64)]
    unnamed x16 -> x0, local copies, waits for them, and re-layouts: 2.76 us -> none
    slice x0 -> x1, local copies, waits for them, and re-layouts: none -> 1.54 us  [body(): return (out[:4], out[4:])]
where the time goes in v2:
time: 116 us
  Pallas kernels  113 us (97%)
  local copies, waits for them, and re-layouts  1.54 us (1%)
    pallas_call x1, Pallas kernels, body(): pl.pallas_call(kernel, out_shape=jax.ShapeDtypeStruct((8, D), BF16), in_s...  113 us

profile of v2, /device:TPU:1, one launch (start us, length us, event | category | flops | bytes accessed | tf_op | source)
XLA Modules:
  0.0 115.5 jit_solution(17592099016686847144)
XLA Ops:
  0.6 113.3 %step.1 = bf16[8,3584]{1,0:T(8,128)(2,1)} custom-call(s32[1,4,8]{2,1,0:T(4,128)} %bitcast.7, bf16[48]{0:T(256)(128)(2,1)} %ps_hbm.1, s32[2]{0:T(128)} %len_hbm.1, s32[2,32]{1,0:T(2,128)} %pt_hbm.1, bf16[48,64,512]{2,1,0:T(8,128)(2,1)} %lat_hbm.1, bf16[48,4096]{1,0:T(8,128)(2,1)} %rope_hbm.1, bf16[256,512]{1,0:T(8,128)(2,1)} %bitcast.4, ...), custom_call_target="tpu_custom_call" | custom-call | tf_op jit(solution)/shard_map/step/pallas_call | solution.py:547
  114.0 1.5 %fusion = (bf16[4,3584]{1,0:T(4,128)(2,1)}, bf16[4,3584]{1,0:T(4,128)(2,1)}) fusion(bf16[8,3584]{1,0:T(8,128)(2,1)} %step.1), kind=kLoop, calls=%fused_computation | loop fusion | bytes 114688 | tf_op jit(solution)/shard_map/slice | solution.py:578

commit v3 on v2

--- a/solution.py
+++ b/solution.py
@@ -39,8 +39,8 @@
     lat_v, wuv, wout, wg, wu, wd,
     slat, srope, rlat, rrope, newk, newr, q_l, q_r, m_s, l_s, o_s,
     so, ro, s_f, d_f, sp2, pr2, al_f, res_l, gain_l,
-    q_s, qt_s, sd, rd, t_f, xr, pp, sr, ss, hb, hr, fb, fr, sret, rret,
-    lsem, pg_s, pg_r, w_ss, w_rs, o_ss, o_rs, p2_s, p2_r, d_ss, d_rs, ag_s, ag_r, rs_s, rs_r, b_ss, b_rs,
+    q_s, qt_s, c_s, sd, rd, t_f, xr, pp, sr, ss, hb, hr, fb, fr, sret, rret,
+    lsem, pg_s, pg_r, w_ss, w_rs, o_ss, o_rs, p2_s, p2_r, d_ss, d_rs, ag_s, ag_r, rs_s, rs_r, b_ss, b_rs, met,
 ):
     i = lax.axis_index("dp")
     j = lax.axis_index("expert")
@@ -64,22 +64,31 @@
     def _(k):
         pl.semaphore_signal(barrier, inc=1, device_id=dp_to(k // 2, k % 2), device_id_type=MESH)
 
+    near = ((1, 0), (-1, 0), (0, 1), (0, -1))
+    for dy, dz in near:
+        pl.semaphore_signal(barrier, inc=1, device_id=(i, ex_at(dy, dz)), device_id_type=MESH)
+
+    rounds = (near, ((0, 2), (0, -2)), ((0, 4), (0, 1), (0, -1)))
+
+    def tell(n):
+        for dy, dz in rounds[n]:
+            pl.semaphore_signal(met.at[n], inc=1, device_id=(i, ex_at(dy, dz)), device_id_type=MESH)
+
+    def hear(n):
+        pl.semaphore_wait(met.at[n], len(rounds[n]))
+
     pairs = [
-        (mv_hbm.at[0], mv_ref), (ps_hbm, ps_ref), (lat_hbm, lat_v), (rope_hbm, rope_raw), (wuv_hbm, wuv.at[0]),
-        (wout_hbm, wout.at[0]), (len_hbm, len_ref), (pt_hbm, pt_ref), (q_hbm, q_ref), (qr_hbm, qr_ref),
+        (mv_hbm.at[0], mv_ref), (lat_hbm, lat_v), (wuv_hbm, wuv.at[0]), (wout_hbm, wout.at[0]), (ps_hbm, ps_ref),
+        (rope_hbm, rope_raw), (len_hbm, len_ref), (pt_hbm, pt_ref), (q_hbm, q_ref), (qr_hbm, qr_ref),
         (nl_hbm, nl_ref), (nr_hbm, nr_ref), (rt_hbm, rt_ref), (res_hbm, res_ref), (gain_hbm, gain_ref),
         (wr_hbm, wr_ref), (wg_hbm.at[0], wg), (wu_hbm.at[0], wu), (wd_hbm.at[0], wd),
     ]
     loads = [pltpu.make_async_copy(a, b, lsem.at[n]) for n, (a, b) in enumerate(pairs)]
-    for cp in loads:
+    for cp in loads[:16]:
         cp.start()
 
-    @pl.loop(1, 32)
-    def _(k):
-        pl.semaphore_signal(barrier, inc=1, device_id=(i, ex_at(k // 8, k % 8)), device_id_type=MESH)
-
-    for n in range(3):
-        loads[n].wait()
+    loads[0].wait()
+    loads[1].wait()
 
     def dest_of(k):
         return ((x + k // 2) % 4) * 2 + (c + k % 2) % 2
@@ -121,19 +130,24 @@
         ][n]
         return rcopy(src, dst, w_ss.at[kind, n], w_rs.at[kind, n], dev)
 
-    pl.semaphore_wait(barrier, 38)
-
-    @pl.loop(1, 8)
-    def _(k):
-        page_copy(k, 0).start()
-
-    loads[4].wait()
-    loads[5].wait()
+    pl.semaphore_wait(barrier, 11)
+    tell(0)
+
+    loads[2].wait()
+    loads[3].wait()
     for kind in range(3):
         w_copy(kind, 0).start()
         w_copy(kind, 1).start()
-
-    loads[3].wait()
+    for k in (4, 5, 2, 6, 3, 7, 1):
+        page_copy(k, 0).start()
+    for cp in loads[16:]:
+        cp.start()
+
+    hear(0)
+    tell(1)
+
+    loads[4].wait()
+    loads[5].wait()
     low48 = iota((48, 128), 1) < 64
     for g in range(32):
         v = rope_raw[:, g * 128 : (g + 1) * 128].astype(F32)
@@ -168,9 +182,11 @@
         second = jnp.where(low16, scales[2], scales[3])
         srope[k, 128:144, :] = jnp.where(row16 == 0, first, second).astype(BF16)
 
-    @pl.loop(1, 8)
-    def _(k):
+    for k in (4, 5, 2, 6, 3, 7, 1):
         page_copy(k, 1).start()
+
+    hear(1)
+    tell(2)
 
     for n in range(6, 16):
         loads[n].wait()
@@ -212,6 +228,8 @@
         res_l[4 * k : 4 * k + 4, :] = res_ref[:, k * CH : (k + 1) * CH].astype(F32)
         gain_l[4 * k : 4 * k + 4, :] = jnp.broadcast_to(gain_ref[k * CH : (k + 1) * CH].reshape(1, CH), (4, CH))
 
+    hear(2)
+
     zeros64 = jnp.zeros((256, 64), F32)
     qr = qr_ref[...].astype(F32)
     q_l[...] = jnp.concatenate([qr, zeros64], axis=1).astype(BF16)
@@ -284,15 +302,15 @@
     moved_from(1)
     pass_on(1)
 
-    @pl.loop(2, 4)
+    @pl.loop(4, 6)
     def _(k):
         moved_from(k)
 
     pass_on(2)
 
-    @pl.loop(4, 8)
-    def _(k):
-        moved_from(k)
+    @pl.loop(0, 4)
+    def _(n):
+        moved_from(2 + (n % 2) * 4 + n // 2)
 
     o = (o_s[...] / l_s[:, 0:1]).astype(BF16)
     pr = iota((256, 256), 0)
@@ -325,23 +343,26 @@
     hv = dot(fold, hv).astype(BF16)
     for kind, n in ((1, 4), (1, 5), (1, 6), (2, 4), (2, 5)):
         w_copy(kind, n).wait_recv()
-    for k in range(NK):
-        w = slice(k * CH, (k + 1) * CH)
-        s_f[:, w] = sum(dot(hv[:, d * 256 : (d + 1) * 256], wout[d, :, w]) for d in range(4))
-    for zz in range(8):
-        for k in range(NK):
-            d_f[zz, 4 * k : 4 * k + 4, :] = s_f[4 * zz : 4 * zz + 4, k * CH : (k + 1) * CH]
-    sp2[...] = d_f[...].astype(BF16)
-
-    def z_copy(n):
-        zz = (z + n) % 8
-        return rcopy(sp2.at[zz], pr2.at[n], p2_s.at[n], p2_r.at[n], (i, ex_at(0, n)))
-
-    for n in (4, 3, 5, 2, 6, 1, 7):
-        z_copy(n).start()
+    def z_copy(n, part):
+        rows = pl.ds(part * 16, 16)
+        return rcopy(
+            sp2.at[(z + n) % 8, rows], pr2.at[n, rows], p2_s.at[part, n], p2_r.at[part, n], (i, ex_at(0, n))
+        )
+
+    far_first = (4, 3, 5, 2, 6, 1, 7)
+    for part in range(2):
+        for k in range(4 * part, min(4 * part + 4, NK)):
+            w = slice(k * CH, (k + 1) * CH)
+            s_f[:, w] = sum(dot(hv[:, d * 256 : (d + 1) * 256], wout[d, :, w]) for d in range(4))
+            for zz in range(8):
+                d_f[zz, 4 * k : 4 * k + 4, :] = s_f[4 * zz : 4 * zz + 4, w]
+        sp2[:, 16 * part : 16 * part + 16, :] = d_f[:, 16 * part : 16 * part + 16, :].astype(BF16)
+        for n in far_first:
+            z_copy(n, part).start()
     total = d_f[z]
     for n in range(1, 8):
-        z_copy(n).wait_recv()
+        z_copy(n, 0).wait_recv()
+        z_copy(n, 1).wait_recv()
         total = total + pr2[n].astype(F32)
     al_f[...] = total
 
@@ -371,8 +392,8 @@
     gates = ROUTE_SCALE * sig / jnp.sum(sig, -1, keepdims=True)
     g_hi = gates.astype(BF16)
     g_lo = (gates - g_hi.astype(F32)).astype(BF16)
-    c_hi = (dot(g_hi, spread) * qt_s[...]).astype(BF16)
-    c_lo = (dot(g_lo, spread) * qt_s[...]).astype(BF16)
+    c_s[0] = (dot(g_hi, spread) * qt_s[...]).astype(BF16)
+    c_s[1] = (dot(g_lo, spread) * qt_s[...]).astype(BF16)
     for k in range(NK):
         out_ref[0:4, k * CH : (k + 1) * CH] = al_f[4 * k : 4 * k + 4, :].astype(BF16)
     for n in range(16, 19):
@@ -496,24 +517,10 @@
 
     rret[j] = sret[0]
 
-    @pl.loop(1, 32)
-    def _(k):
-        b_copy(k).wait_recv()
-
-    rows = rret[...].reshape(512, CH)
-    al_f[...] = dot(c_hi, rows) + dot(c_lo, rows)
-    for k in range(NK):
-        out_ref[4:8, k * CH : (k + 1) * CH] = al_f[4 * k : 4 * k + 4, :].astype(BF16)
-
     @pl.loop(1, 8)
     def _(k):
         page_copy(k, 0).wait_send()
         page_copy(k, 1).wait_send()
-
-    @pl.loop(1, 32)
-    def _(k):
-        d_copy(k).wait_send()
-        b_copy(k).wait_send()
 
     for kind in range(3):
         for n in range(7):
@@ -521,7 +528,8 @@
                 w_copy(kind, n).wait_send()
     for n in range(1, 8):
         o_copy(n).wait_send()
-        z_copy(n).wait_send()
+        z_copy(n, 0).wait_send()
+        z_copy(n, 1).wait_send()
 
     @pl.loop(0, 4)
     def _(g):
@@ -529,6 +537,23 @@
             ag(g, n).wait_send()
         for n in range(5):
             rs(g, n).wait_send()
+
+    @pl.loop(1, 32)
+    def _(k):
+        d_copy(k).wait_send()
+        b_copy(k).wait_send()
+
+    al_f[...] = jnp.zeros_like(al_f)
+    for g in range(4):
+        for n in range(8):
+            if g * 8 + n:
+                b_copy(g * 8 + n).wait_recv()
+        group = (y + g) % 4
+        rows = rret[pl.ds(group * 8, 8)].reshape(128, CH)
+        lanes = pl.ds(pl.multiple_of(group * 128, 128), 128)
+        al_f[...] += dot(c_s[0, :, lanes], rows) + dot(c_s[1, :, lanes], rows)
+    for k in range(NK):
+        out_ref[4:8, k * CH : (k + 1) * CH] = al_f[4 * k : 4 * k + 4, :].astype(BF16)
 
 
 def body(
@@ -562,13 +587,13 @@
             vm((8, 32, CH), BF16), vm((8, 32, CH), BF16), vm((32, D), F32),
             vm((8, 32, CH), F32), vm((8, 32, CH), BF16), vm((8, 32, CH), BF16),
             vm((32, CH), F32), vm((32, CH), F32), vm((32, CH), F32),
-            vm((512, 32), BF16), vm((32, 512), F32), vm((32, 16, CH), BF16), vm((32, 16, CH), BF16),
+            vm((512, 32), BF16), vm((32, 512), F32), vm((2, 32, 512), BF16), vm((32, 16, CH), BF16), vm((32, 16, CH), BF16),
             vm((512, 128), F32), vm((4, 8, 16, D), BF16), vm((4, 8, 16, D), BF16), vm((4, 4, 16, D), BF16),
             vm((4, 4, 16, D), F32), vm((4, 16, D), BF16), vm((4, 2, 16, HALF), BF16),
             vm((4, 2, 16, D), BF16), vm((4, 2, 16, D), BF16), vm((32, 16, CH), BF16), vm((32, 16, CH), BF16),
             dma((19,)), dma((2, 8)), dma((2, 8)), dma((3, 7)), dma((3, 7)), dma((8,)), dma((8,)),
-            dma((8,)), dma((8,)), dma((32,)), dma((32,)), dma((4, 8)), dma((4, 8)), dma((4, 5)), dma((4, 5)),
-            dma((32,)), dma((32,)),
+            dma((2, 8)), dma((2, 8)), dma((32,)), dma((32,)), dma((4, 8)), dma((4, 8)), dma((4, 5)), dma((4, 5)),
+            dma((32,)), dma((32,)), pltpu.SemaphoreType.REGULAR((3,)),
         ],
         compiler_params=pltpu.CompilerParams(
             collective_id=0, has_side_effects=True, vmem_limit_bytes=60 * 2**20

time: 116 us -> 114 us (0.983)
  Pallas kernels: 113 us -> 111 us
    pallas_call x1, Pallas kernels: 113 us -> 111 us  [body(): pl.pallas_call(kernel, out_shape=jax.ShapeDtypeStruct((8, D), BF16), in_s...]
where the time goes in v3:
time: 114 us; the launch traced here: 113 us
  Pallas kernels  111 us (97%)
  local copies, waits for them, and re-layouts  1.54 us (1%)
    pallas_call x1, Pallas kernels, body(): pl.pallas_call(kernel, out_shape=jax.ShapeDtypeStruct((8, D), BF16), in_s...  111 us

profile of v3, /device:TPU:1, one launch (start us, length us, event | category | flops | bytes accessed | tf_op | source)
XLA Modules:
  0.0 113.3 jit_solution(10716716716935467230)
XLA Ops:
  0.6 111.1 %step.1 = bf16[8,3584]{1,0:T(8,128)(2,1)} custom-call(s32[1,4,8]{2,1,0:T(4,128)} %bitcast.7, bf16[48]{0:T(256)(128)(2,1)} %ps_hbm.1, s32[2]{0:T(128)} %len_hbm.1, s32[2,32]{1,0:T(2,128)} %pt_hbm.1, bf16[48,64,512]{2,1,0:T(8,128)(2,1)} %lat_hbm.1, bf16[48,4096]{1,0:T(8,128)(2,1)} %rope_hbm.1, bf16[256,512]{1,0:T(8,128)(2,1)} %bitcast.4, ...), custom_call_target="tpu_custom_call" | custom-call | tf_op jit(solution)/shard_map/step/pallas_call | solution.py:572
  111.8 1.5 %fusion = (bf16[4,3584]{1,0:T(4,128)(2,1)}, bf16[4,3584]{1,0:T(4,128)(2,1)}) fusion(bf16[8,3584]{1,0:T(8,128)(2,1)} %step.1), kind=kLoop, calls=%fused_computation | loop fusion | bytes 114688 | tf_op jit(solution)/shard_map/slice | solution.py:603

commit v4 on v3

--- a/solution.py
+++ b/solution.py
@@ -138,8 +138,8 @@
     for kind in range(3):
         w_copy(kind, 0).start()
         w_copy(kind, 1).start()
-    for k in (4, 5, 2, 6, 3, 7, 1):
-        page_copy(k, 0).start()
+    page_copy(4, 0).start()
+    page_copy(5, 0).start()
     for cp in loads[16:]:
         cp.start()
 
@@ -182,7 +182,10 @@
         second = jnp.where(low16, scales[2], scales[3])
         srope[k, 128:144, :] = jnp.where(row16 == 0, first, second).astype(BF16)
 
-    for k in (4, 5, 2, 6, 3, 7, 1):
+    page_copy(4, 1).start()
+    page_copy(5, 1).start()
+    for k in (2, 6, 3, 7, 1):
+        page_copy(k, 0).start()
         page_copy(k, 1).start()
 
     hear(1)
@@ -299,7 +302,6 @@
         w_copy(kind, 5).start()
 
     pass_on(0)
-    moved_from(1)
     pass_on(1)
 
     @pl.loop(4, 6)
@@ -307,6 +309,8 @@
         moved_from(k)
 
     pass_on(2)
+
+    moved_from(1)
 
     @pl.loop(0, 4)
     def _(n):
@@ -377,9 +381,10 @@
         e = ex_at(k // 8, k % 8)
         return rcopy(sd.at[e], rd.at[k], d_ss.at[k], d_rs.at[k], (i, e))
 
-    @pl.loop(1, 32)
-    def _(k):
-        d_copy(k).start()
+    for dy in range(4):
+        for dz in (4, 3, 5, 2, 6, 1, 7, 0):
+            if dy or dz:
+                d_copy(dy * 8 + dz).start()
 
     rd[0] = sd[j]
 
@@ -402,14 +407,16 @@
     def ag(g, n):
         lo, hi = pl.ds(0, HALF), pl.ds(HALF, HALF)
         src, dst, dev = [
-            (xr.at[g, 0], xr.at[g, 3], right),
-            (xr.at[g, 0], xr.at[g, 1], left),
+            (xr.at[g, 0, :, lo], xr.at[g, 3, :, lo], right),
+            (xr.at[g, 0, :, hi], xr.at[g, 1, :, hi], left),
             (xr.at[g, 3, :, lo], xr.at[g, 2, :, lo], right),
             (xr.at[g, 1, :, hi], xr.at[g, 2, :, hi], left),
             (xr.at[g, 0], xr.at[g, 4], sib),
             (xr.at[g, 3], xr.at[g, 7], sib),
             (xr.at[g, 1], xr.at[g, 5], sib),
             (xr.at[g, 2], xr.at[g, 6], sib),
+            (xr.at[g, 0, :, hi], xr.at[g, 3, :, hi], right),
+            (xr.at[g, 0, :, lo], xr.at[g, 1, :, lo], left),
         ][n]
         return rcopy(src, dst, ag_s.at[g, n], ag_r.at[g, n], dev)
 
@@ -419,8 +426,10 @@
             (pp.at[g, pl.ds(4, 4)], sr.at[g], sib),
             (hb.at[g, :, lo], hr.at[g, 0], right),
             (hb.at[g, :, hi], hr.at[g, 1], left),
-            (fb.at[g, 0], fr.at[g, 0], right),
-            (fb.at[g, 1], fr.at[g, 1], left),
+            (fb.at[g, 0, :, hi], fr.at[g, 0, :, hi], right),
+            (fb.at[g, 1, :, lo], fr.at[g, 1, :, lo], left),
+            (fb.at[g, 0, :, lo], fr.at[g, 0, :, lo], right),
+            (fb.at[g, 1, :, hi], fr.at[g, 1, :, hi], left),
         ][n]
         return rcopy(src, dst, rs_s.at[g, n], rs_r.at[g, n], dev)
 
@@ -442,15 +451,17 @@
             for b in range(4):
                 at = k * CH + b * 128
                 xr[g, 0, :, at : at + 128] = t_f[pl.ds(b * 128 + k, 16, stride=8), :].astype(BF16)
-        for n in (0, 1, 4):
+        for n in (0, 1, 8, 9, 4):
             ag(g, n).start()
 
     def stage_b(g):
         ag(g, 0).wait_recv()
         ag(g, 2).start()
-        ag(g, 5).start()
         ag(g, 1).wait_recv()
         ag(g, 3).start()
+        ag(g, 8).wait_recv()
+        ag(g, 5).start()
+        ag(g, 9).wait_recv()
         ag(g, 6).start()
 
     def stage_c(g):
@@ -472,24 +483,26 @@
 
     def stage_e(g):
         rs(g, 0).wait_recv()
-        ss[g] = pp[g, 0:4].astype(F32) + sr[g].astype(F32)
-        hb[g] = ss[g, 2].astype(BF16)
+        hb[g] = (pp[g, 2].astype(F32) + sr[g, 2].astype(F32)).astype(BF16)
         rs(g, 1).start()
         rs(g, 2).start()
+        ss[g] = pp[g, 0:4].astype(F32) + sr[g].astype(F32)
+        fb[g, 0, :, HALF:] = ss[g, 1, :, HALF:].astype(BF16)
+        fb[g, 1, :, 0:HALF] = ss[g, 3, :, 0:HALF].astype(BF16)
+        rs(g, 3).start()
+        rs(g, 4).start()
 
     def stage_f(g):
         rs(g, 1).wait_recv()
         fb[g, 0, :, 0:HALF] = (ss[g, 1, :, 0:HALF] + hr[g, 0].astype(F32)).astype(BF16)
-        fb[g, 0, :, HALF:] = ss[g, 1, :, HALF:].astype(BF16)
-        rs(g, 3).start()
+        rs(g, 5).start()
         rs(g, 2).wait_recv()
-        fb[g, 1, :, 0:HALF] = ss[g, 3, :, 0:HALF].astype(BF16)
         fb[g, 1, :, HALF:] = (ss[g, 3, :, HALF:] + hr[g, 1].astype(F32)).astype(BF16)
-        rs(g, 4).start()
+        rs(g, 6).start()
 
     def stage_g(g):
-        rs(g, 3).wait_recv()
-        rs(g, 4).wait_recv()
+        for n in range(3, 7):
+            rs(g, n).wait_recv()
         for b in range(4):
             for k in range(NK):
                 w = slice(k * CH + b * 128, k * CH + b * 128 + 128)
@@ -499,11 +512,12 @@
         back = jnp.concatenate([t_f[b * 128 : (b + 1) * 128, :] for b in range(4)], axis=1)
         sret[pl.ds(g * 8, 8)] = back.astype(BF16).reshape(8, 16, CH)
 
-        @pl.loop(0, 8)
-        def _(n):
-            @pl.when(g * 8 + n > 0)
-            def _():
-                b_copy(g * 8 + n).start()
+        for n in (4, 3, 5, 2, 6, 1, 7):
+            b_copy(g * 8 + n).start()
+
+        @pl.when(g > 0)
+        def _():
+            b_copy(g * 8).start()
 
     stages = [(stage_a, 0), (stage_b, 1), (stage_c, 2), (stage_d, 2), (stage_e, 3), (stage_f, 4), (stage_g, 5)]
 
@@ -533,9 +547,9 @@
 
     @pl.loop(0, 4)
     def _(g):
-        for n in range(8):
+        for n in range(10):
             ag(g, n).wait_send()
-        for n in range(5):
+        for n in range(7):
             rs(g, n).wait_send()
 
     @pl.loop(1, 32)
@@ -571,7 +585,7 @@
     )
     out = pl.pallas_call(
         kernel,
-        out_shape=jax.ShapeDtypeStruct((8, D), BF16),
+        out_shape=pltpu.VMEM((8, D), BF16),
         in_specs=[any_spec] * len(operands),
         out_specs=vmem,
         scratch_shapes=[
@@ -592,7 +606,7 @@
             vm((4, 4, 16, D), F32), vm((4, 16, D), BF16), vm((4, 2, 16, HALF), BF16),
             vm((4, 2, 16, D), BF16), vm((4, 2, 16, D), BF16), vm((32, 16, CH), BF16), vm((32, 16, CH), BF16),
             dma((19,)), dma((2, 8)), dma((2, 8)), dma((3, 7)), dma((3, 7)), dma((8,)), dma((8,)),
-            dma((2, 8)), dma((2, 8)), dma((32,)), dma((32,)), dma((4, 8)), dma((4, 8)), dma((4, 5)), dma((4, 5)),
+            dma((2, 8)), dma((2, 8)), dma((32,)), dma((32,)), dma((4, 10)), dma((4, 10)), dma((4, 7)), dma((4, 7)),
             dma((32,)), dma((32,)), pltpu.SemaphoreType.REGULAR((3,)),
         ],
         compiler_params=pltpu.CompilerParams(

time: 114 us -> 111 us (0.974)
  Pallas kernels: 111 us -> 109 us
    pallas_call x1, Pallas kernels: 111 us -> 109 us  [body(): pl.pallas_call(kernel, out_shape=pltpu.VMEM((8, D), BF16), in_specs=[any_...]
where the time goes in v4:
time: 111 us
  Pallas kernels  109 us (98%)
    pallas_call x1, Pallas kernels, body(): pl.pallas_call(kernel, out_shape=pltpu.VMEM((8, D), BF16), in_specs=[any_...  109 us

profile of v4, /device:TPU:1, one launch (start us, length us, event | category | flops | bytes accessed | tf_op | source)
XLA Modules:
  0.0 110.6 jit_solution(12586939684684963914)
XLA Ops:
  0.6 109.4 %step.1 = bf16[8,3584]{1,0:T(8,128)(2,1)S(1)} custom-call(s32[1,4,8]{2,1,0:T(4,128)} %bitcast.7, bf16[48]{0:T(256)(128)(2,1)} %ps_hbm.1, s32[2]{0:T(128)} %len_hbm.1, s32[2,32]{1,0:T(2,128)} %pt_hbm.1, bf16[48,64,512]{2,1,0:T(8,128)(2,1)} %lat_hbm.1, bf16[48,4096]{1,0:T(8,128)(2,1)} %rope_hbm.1, bf16[256,512]{1,0:T(8,128)(2,1)} %bitcast.4, ...), custom_call_target="tpu_custom_call" | custom-call | tf_op jit(solution)/shard_map/step/pallas_call | solution.py:586
  110.0 0.6 fusion

commit v5 on v4

--- a/solution.py
+++ b/solution.py
@@ -133,13 +133,13 @@
     pl.semaphore_wait(barrier, 11)
     tell(0)
 
+    page_copy(4, 0).start()
+    page_copy(5, 0).start()
     loads[2].wait()
     loads[3].wait()
     for kind in range(3):
         w_copy(kind, 0).start()
         w_copy(kind, 1).start()
-    page_copy(4, 0).start()
-    page_copy(5, 0).start()
     for cp in loads[16:]:
         cp.start()
 

time: 111 us -> 111 us (level)
  no operation moved by 1% of the time
where the time goes in v5:
time: 111 us
  Pallas kernels  109 us (98%)
    pallas_call x1, Pallas kernels, body(): pl.pallas_call(kernel, out_shape=pltpu.VMEM((8, D), BF16), in_specs=[any_...  109 us

profile of v5, /device:TPU:1, one launch (start us, length us, event | category | flops | bytes accessed | tf_op | source)
XLA Modules:
  0.0 110.7 jit_solution(11174544686570408849)
XLA Ops:
  0.6 109.4 %step.1 = bf16[8,3584]{1,0:T(8,128)(2,1)S(1)} custom-call(s32[1,4,8]{2,1,0:T(4,128)} %bitcast.7, bf16[48]{0:T(256)(128)(2,1)} %ps_hbm.1, s32[2]{0:T(128)} %len_hbm.1, s32[2,32]{1,0:T(2,128)} %pt_hbm.1, bf16[48,64,512]{2,1,0:T(8,128)(2,1)} %lat_hbm.1, bf16[48,4096]{1,0:T(8,128)(2,1)} %rope_hbm.1, bf16[256,512]{1,0:T(8,128)(2,1)} %bitcast.4, ...), custom_call_target="tpu_custom_call" | custom-call | tf_op jit(solution)/shard_map/step/pallas_call | solution.py:586
  110.0 0.6 fusion
